TPU v7x, 32 devices: a whole 2x2x4 slice. The times are simulated.
32 devices in a mesh: users: 8 (over z, x), items: 4 (over y, core).
Axes of the slice: x: 2, y: 2, z: 4, core: 2. Of those that a mesh axis runs over, the one named last changes fastest.
Arguments:
- user_factors: bfloat16 [65536, 256], P(('users', 'items')), may hold values from -1.5 to 1.5
- item_factors: bfloat16 [1024, 256], P('items'), may hold values from -1.5 to 1.5
- block_user: int32 [32, 128], P(('users', 'items')), may hold values from 0 to 15
- block_item: int32 [32, 128], P(('users', 'items')), may hold values from 0 to 7
- counts: int32 [32], P(('users', 'items')), may hold values from 1 to 128, as said below
- ratings: bfloat16 [32, 128, 128, 128], P(('users', 'items')), may hold values from -6 to 6
- weights: bfloat16 [32, 128, 128, 128], P(('users', 'items')), may hold values from 0 to 4
Outputs:
- user_grad: float32 [65536, 256], P(('users', 'items'))
- item_grad: float32 [1024, 256], P(('users', 'items'))
Inputs may be any that keep to these rules, and one draw needn't show every extreme that they name: counts[g] live slots come first on device g; later slots are ignored; some device has exactly 128 and some device exactly 1.
All inputs are finite; a program needn't handle non-finite values.
Results may differ from a plain program's by a relative error of at most 0.0022.
Values may be sent and summed in bfloat16 or wider, within the bound.
No kernel may reach another device: no remote copies, remote signals or barrier semaphores. Data moves between devices by JAX's collectives and lax.ppermute only.
A program may use at most 64 MiB of HBM per device.

v0:
```python
import jax
import jax.numpy as jnp
from jax import lax
from jax.sharding import PartitionSpec as P

grad_scale = 0.015625
decay_rate = 0.05


def select_tiles(selector, tiles):
    picked = jnp.einsum(
        "gb,bur->gur", selector.astype(jnp.bfloat16), tiles, preferred_element_type=jnp.float32
    )
    return picked.astype(jnp.bfloat16)


def add_tiles(total, selector, terms):
    return total + jnp.einsum(
        "gb,gur->bur",
        selector,
        terms,
        precision=lax.Precision.HIGHEST,
        preferred_element_type=jnp.float32,
    )


def body(user_factors, item_factors, block_user, block_item, counts, ratings, weights):
    rank_width = user_factors.shape[1]
    block_width = ratings.shape[2]
    user_slab = user_factors.reshape(-1, block_width, rank_width)
    item_whole = lax.all_gather(item_factors, "items", axis=0, tiled=True)
    item_blocks = item_whole.reshape(-1, block_width, rank_width)
    user_block_total = user_slab.shape[0]
    item_block_total = item_blocks.shape[0]
    slot_total = ratings.shape[1]
    group_size = min(slot_total, 8)
    live_count = counts[0]
    turn_total = (live_count + group_size - 1) // group_size
    slot_offsets = jnp.arange(group_size, dtype=jnp.int32)
    user_range = jnp.arange(user_block_total, dtype=jnp.int32)
    item_range = jnp.arange(item_block_total, dtype=jnp.int32)

    def group_terms(turn_index):
        first_slot = turn_index * group_size
        user_ids = lax.dynamic_slice_in_dim(block_user[0], first_slot, group_size, 0)
        item_ids = lax.dynamic_slice_in_dim(block_item[0], first_slot, group_size, 0)
        rating_rows = lax.dynamic_slice_in_dim(ratings[0], first_slot, group_size, 0)
        weight_rows = lax.dynamic_slice_in_dim(weights[0], first_slot, group_size, 0)
        live_rows = first_slot + slot_offsets < live_count
        user_select = (user_ids[:, None] == user_range[None, :]).astype(jnp.float32)
        item_select = (item_ids[:, None] == item_range[None, :]).astype(jnp.float32)
        user_tiles = select_tiles(user_select, user_slab)
        item_tiles = select_tiles(item_select, item_blocks)
        predicted = jnp.einsum(
            "gur,gir->gui", user_tiles, item_tiles, preferred_element_type=jnp.float32
        )
        weighted = weight_rows.astype(jnp.float32) * (predicted - rating_rows.astype(jnp.float32))
        weighted = jnp.where(live_rows[:, None, None], weighted, 0.0).astype(jnp.bfloat16)
        return (user_select, item_select, user_tiles, item_tiles, weighted)

    def both_update(turn_index, carry):
        user_acc, item_acc = carry
        user_select, item_select, user_tiles, item_tiles, weighted = group_terms(turn_index)
        user_terms = jnp.einsum(
            "gui,gir->gur", weighted, item_tiles, preferred_element_type=jnp.float32
        )
        item_terms = jnp.einsum(
            "gui,gur->gir", weighted, user_tiles, preferred_element_type=jnp.float32
        )
        return (
            add_tiles(user_acc, user_select, user_terms),
            add_tiles(item_acc, item_select, item_terms),
        )

    user_zero = jnp.zeros(user_slab.shape, jnp.float32)
    item_zero = jnp.zeros(item_blocks.shape, jnp.float32)
    user_acc, item_acc = lax.fori_loop(0, turn_total, both_update, (user_zero, item_zero))
    summed = lax.psum_scatter(
        item_acc.reshape(-1, rank_width), ("users", "items"), scatter_dimension=0, tiled=True
    )
    owned_rows = summed.shape[0]
    owner_index = lax.axis_index("users") * lax.axis_size("items") + lax.axis_index("items")
    own_factors = lax.dynamic_slice_in_dim(item_whole, owner_index * owned_rows, owned_rows, 0)
    item_grad = summed * grad_scale + decay_rate * own_factors.astype(jnp.float32)
    user_grad = user_acc.reshape(-1, rank_width) * grad_scale + decay_rate * user_factors.astype(
        jnp.float32
    )
    return (user_grad, item_grad)


def solution(mesh):
    in_specs = (
        P(("users", "items"), None),
        P("items", None),
        P(("users", "items"), None),
        P(("users", "items"), None),
        P(("users", "items")),
        P(("users", "items"), None, None, None),
        P(("users", "items"), None, None, None),
    )
    out_specs = (P(("users", "items"), None), P(("users", "items"), None))
    return jax.shard_map(body, mesh=mesh, in_specs=in_specs, out_specs=out_specs, check_vma=False)
```

profile of v0, /device:TPU:0, one launch (start us, length us, event | category | flops | bytes accessed | tf_op | source)
XLA Modules:
  0.0 312.0 jit_solution(4771320075359831687)
XLA Ops:
  8.0 8.9 %all_gather.3 = bf16[1024,256]{1,0:T(8,128)(2,1)S(1)} all-gather(bf16[256,256]{1,0:T(8,128)(2,1)} %param.10), channel_id=1, replica_groups=mesh['users'=8,'items'=4] {'items'}, dimensions={0}, use_global_device_ids=true | all-gather | bytes 655360 | tf_op jit(solution)/shard_map/all_gather | solution.py:31
  17.9 1.6 copy.18
  20.1 138.8 %while.15 = (s32[]{:T(128)}, f32[16,128,256]{2,0,1:T(8,128)S(1)}, f32[8,128,256]{2,0,1:T(8,128)S(1)}, s32[]{:T(128)}, s32[1,128]{1,0:T(1,128)S(1)}, /*index=5*/s...) while((s32[]{:T(128)}, f32[16,128,256]{2,0,1:T(8,128)S(1)}, ...), condition=%wide.region_1.2_spmd.clone.clone, body=%wide.region_0.1_spmd.clone.clone.sunk | while | flops 291504928 | bytes 16515547 | solution.py:77
  20.9 1.4 convolution_convert_fusion.4
  22.3 1.6 convolution_convert_fusion.5
  27.2 2.2 convolution_add_fusion.4
  30.1 1.4 convolution_convert_fusion.4
  31.5 1.6 convolution_convert_fusion.5
  36.4 2.2 convolution_add_fusion.4
  39.4 1.4 convolution_convert_fusion.4
  40.8 1.6 convolution_convert_fusion.5
  45.7 2.2 convolution_add_fusion.4
  48.6 1.4 convolution_convert_fusion.4
  50.0 1.6 convolution_convert_fusion.5
  54.9 2.2 convolution_add_fusion.4
  57.9 1.4 convolution_convert_fusion.4
  59.3 1.6 convolution_convert_fusion.5
  64.2 2.2 convolution_add_fusion.4
  67.1 1.4 convolution_convert_fusion.4
  68.5 1.6 convolution_convert_fusion.5
  73.4 2.2 convolution_add_fusion.4
  76.4 1.4 convolution_convert_fusion.4
  77.8 1.6 convolution_convert_fusion.5
  82.7 2.2 convolution_add_fusion.4
  85.7 1.4 convolution_convert_fusion.4
  87.0 1.6 convolution_convert_fusion.5
  92.0 2.2 convolution_add_fusion.4
  94.9 1.4 convolution_convert_fusion.4
  96.3 1.6 convolution_convert_fusion.5
  101.2 2.2 convolution_add_fusion.4
  104.2 1.4 convolution_convert_fusion.4
  105.6 1.6 convolution_convert_fusion.5
  110.5 2.2 convolution_add_fusion.4
  113.4 1.4 convolution_convert_fusion.4
  114.8 1.6 convolution_convert_fusion.5
  119.7 2.2 convolution_add_fusion.4
  124.1 1.6 convolution_convert_fusion.5
  129.0 2.2 convolution_add_fusion.4
  131.9 1.4 convolution_convert_fusion.4
  133.3 1.6 convolution_convert_fusion.5
  138.2 2.2 convolution_add_fusion.4
  142.6 1.6 convolution_convert_fusion.5
  147.5 2.2 convolution_add_fusion.4
  150.4 1.4 convolution_convert_fusion.4
  151.8 1.6 convolution_convert_fusion.5
  156.7 2.2 convolution_add_fusion.4
  161.7 1.6 bitcast_add_fusion
  163.3 140.4 %reduce-scatter.2.cloned.1.call-done = f32[32,256]{1,0:T(8,128)} async-done(((f32[1024,256]{1,0:T(8,128)}), f32[32,256]{1,0:T(8,128)}) %reduce-scatter.2.cloned.1.call-update) | async-done | bytes 32784 | tf_op jit(solution)/shard_map/reduce_scatter | solution.py:78
  (111 shorter events, 69.3 us)
Async XLA Ops:
  7.2 10.7 %copy-start = (bf16[2048,256]{1,0:T(8,128)(2,1)S(1)}, bf16[2048,256]{1,0:T(8,128)(2,1)}, u32[]{:S(2)}) copy-start(bf16[2048,256]{1,0:T(8,128)(2,1)} %param.9) | copy-start | bytes 3145732
  7.2 296.6 %reduce-scatter.2.cloned.1.call-start = ((), (), s32[]{:S(2)}) async-start(), calls=%async_computation.1 | async-start | bytes 1081344 | tf_op jit(solution)/shard_map/reduce_scatter | solution.py:78
  16.8 2.6 copy-start.2
  19.5 0.7 copy-start.3
  19.5 0.7 copy-start.4
  160.5 1.2 copy-start.1
Sparse Core Ops, SparseCore 0:
  160.4 143.3 reduce-scatter.1
where the time goes:
time: 315 us; the launch traced here: 312 us
  waiting for transfers between devices  140 us (44%)
  matrix products  127 us (40%)
  between operations  14.8 us (5%)
  other arithmetic  13 us (4%)
  blocking collectives  8.86 us (3%)
  local copies, waits for them, and re-layouts  6.97 us (2%)
    reduce_scatter x1, waiting for transfers between devices, body(): lax.psum_scatter(item_acc.reshape(-1, rank_width), ('users', 'items'), sc...  140 us
    dot_general x30, matrix products, add_tiles(): jnp.einsum('gb,gur->bur', selector, terms, precision=lax.Precision.HIGHES...  52.5 us
    dot_general x30, matrix products, select_tiles(): jnp.einsum('gb,bur->gur', selector.astype(jnp.bfloat16), tiles, preferred...  44.5 us
    dot_general x15, matrix products, group_terms(): jnp.einsum('gur,gir->gui', user_tiles, item_tiles, preferred_element_type...  20.4 us
    lt x15, other arithmetic, group_terms(): live_rows = first_slot + slot_offsets < live_count  9.79 us
    all_gather x1, blocking collectives, body(): item_whole = lax.all_gather(item_factors, 'items', axis=0, tiled=True)  8.86 us
  transfers between devices with their start and end apart: 1, of which 1 were waited for; matrix products, arithmetic and copies ran while one was open for 1% of the time, Pallas kernels for 0%

commit v1 on v0

v1 whole, which is shorter than its diff:
```python
import functools

import jax
import jax.numpy as jnp
from jax import lax
from jax.experimental import pallas as pl
from jax.experimental.pallas import tpu as pltpu
from jax.sharding import PartitionSpec as P

grad_scale = 0.015625
decay_rate = 0.05
AXES = ("users", "items")
VMEM = pl.BlockSpec(memory_space=pltpu.VMEM)
SMEM = pl.BlockSpec(memory_space=pltpu.SMEM)
ANY = pl.BlockSpec(memory_space=pl.ANY)


def phases_of(device_total):
    bit_total = device_total.bit_length() - 1
    groups = [[0]]
    for bit in range(1, bit_total, 2):
        groups.append(list(range(bit, min(bit + 2, bit_total))))
    return groups


def place_of(index, groups):
    place = 0
    for group in groups:
        for bit in reversed(group):
            place = place * 2 + ((index >> bit) & 1)
    return place


def item_kernel(unroll, owner_total, groups, count_ref, place_ref, user_id_ref, item_id_ref, user_ref, turned_ref,
                item_ref, rating_ref, weight_ref, keep_ref, send_ref, weighted_ref, total):
    live = count_ref[0]
    block = rating_ref.shape[2]
    total[...] = jnp.zeros_like(total)

    def turn(index, carry):
        base = index * unroll
        predicted = []
        for step in range(unroll):
            user_row = pl.multiple_of(user_id_ref[0, base + step] * block, block)
            item_row = pl.multiple_of(item_id_ref[0, base + step] * block, block)
            predicted.append(lax.dot_general(
                user_ref[pl.ds(user_row, block), :], item_ref[pl.ds(item_row, block), :],
                (((1,), (1,)), ((), ())), preferred_element_type=jnp.float32))
        terms = []
        for step in range(unroll):
            slot = base + step
            weighted = weight_ref[0, slot].astype(jnp.float32) * (
                predicted[step] - rating_ref[0, slot].astype(jnp.float32))
            weighted = jnp.where(slot < live, weighted, 0.0).astype(jnp.bfloat16)
            weighted_ref[slot] = weighted
            terms.append(jnp.dot(turned_ref[user_id_ref[0, slot]], weighted, preferred_element_type=jnp.float32))
        for step in range(unroll):
            total[item_id_ref[0, base + step]] += terms[step]
        return carry

    lax.fori_loop(0, (live + unroll - 1) // unroll, turn, 0)
    own_place = place_ref[0]
    owned = keep_ref.shape[0] * 2 // owner_total
    half = owner_total // 2
    per_block = block // owned
    for item in range(total.shape[0]):
        rows = total[item].T
        for part in range(per_block):
            place = own_place ^ place_of(item * per_block + part, groups)
            piece = rows[part * owned:(part + 1) * owned]
            row = pl.multiple_of((place % half) * owned, owned)

            @pl.when(place < half)
            def _():
                keep_ref[pl.ds(row, owned), :] = piece

            @pl.when(place >= half)
            def _():
                send_ref[pl.ds(row, owned), :] = piece


def user_kernel(unroll, count_ref, user_id_ref, item_id_ref, user_ref, item_ref, weighted_ref, grad_ref, total, sems):
    live = count_ref[0]
    block = weighted_ref.shape[1]
    total[...] = jnp.zeros_like(total)

    def turn(index, carry):
        base = index * unroll
        terms = []
        for step in range(unroll):
            item_row = pl.multiple_of(item_id_ref[0, base + step] * block, block)
            terms.append(jnp.dot(weighted_ref[base + step], item_ref[pl.ds(item_row, block), :],
                                 preferred_element_type=jnp.float32))
        for step in range(unroll):
            user_row = pl.multiple_of(user_id_ref[0, base + step] * block, block)
            total[pl.ds(user_row, block), :] += terms[step]
        return carry

    lax.fori_loop(0, (live + unroll - 1) // unroll, turn, 0)

    def writeback(index):
        rows = pl.ds(index * block, block)
        return pltpu.make_async_copy(total.at[rows], grad_ref.at[rows], sems.at[index])

    blocks = total.shape[0] // block
    for index in range(blocks):
        rows = pl.ds(index * block, block)
        total[rows, :] = total[rows, :] * grad_scale + decay_rate * user_ref[rows, :].astype(jnp.float32)
        writeback(index).start()
    for index in range(blocks):
        writeback(index).wait()


def body(user_factors, item_factors, block_user, block_item, counts, ratings, weights):
    rank = user_factors.shape[1]
    slots, block = ratings.shape[1], ratings.shape[2]
    user_rows = user_factors.shape[0]
    device_total = lax.axis_size(AXES[0]) * lax.axis_size(AXES[1])
    me = lax.axis_index(AXES[0]) * lax.axis_size(AXES[1]) + lax.axis_index(AXES[1])
    groups = phases_of(device_total)
    unroll = 16
    item_whole = lax.all_gather(item_factors, "items", axis=0, tiled=True)
    item_rows = item_whole.shape[0]
    turned = user_factors.reshape(-1, block, rank).swapaxes(1, 2)
    own_place = place_of(me, groups).astype(jnp.int32).reshape(1)
    half_shape = jax.ShapeDtypeStruct((item_rows // 2, rank), jnp.float32)
    keep, send, weighted = pl.pallas_call(
        functools.partial(item_kernel, unroll, device_total, groups),
        out_shape=(half_shape, half_shape, jax.ShapeDtypeStruct((slots, block, block), jnp.bfloat16)),
        in_specs=[SMEM] * 4 + [VMEM] * 5,
        out_specs=(VMEM,) * 3,
        scratch_shapes=[pltpu.VMEM((item_rows // block, rank, block), jnp.float32)],
        compiler_params=pltpu.CompilerParams(vmem_limit_bytes=20 << 20),
        name="item_sums",
    )(counts, own_place, block_user, block_item, user_factors, turned, item_whole, ratings, weights)
    user_grad = pl.pallas_call(
        functools.partial(user_kernel, unroll),
        out_shape=jax.ShapeDtypeStruct((user_rows, rank), jnp.float32),
        in_specs=[SMEM] * 3 + [VMEM] * 3,
        out_specs=ANY,
        scratch_shapes=[pltpu.VMEM((user_rows, rank), jnp.float32), pltpu.SemaphoreType.DMA((user_rows // block,))],
        compiler_params=pltpu.CompilerParams(vmem_limit_bytes=20 << 20),
        cost_estimate=pl.CostEstimate(flops=2 * slots * block * block * rank, bytes_accessed=8 << 20, transcendentals=0),
        name="user_sums",
    )(counts, block_user, block_item, user_factors, item_whole, weighted)

    def permute(array, mask):
        return lax.ppermute(array, AXES, [(index, index ^ mask) for index in range(device_total)])

    partial = keep + permute(send, 1)
    for group in groups[1:]:
        ways = 1 << len(group)
        parts = partial.reshape(ways, -1, rank)
        received = []
        for way in range(1, ways):
            mask = sum(((way >> index) & 1) << bit for index, bit in enumerate(group))
            received.append(permute(parts[way], mask))
        partial = parts[0]
        for array in received:
            partial = partial + array
    owned_rows = partial.shape[0]
    own_factors = lax.dynamic_slice_in_dim(item_whole, me * owned_rows, owned_rows, 0)
    item_grad = partial * grad_scale + decay_rate * own_factors.astype(jnp.float32)
    return (user_grad, item_grad)


def solution(mesh):
    in_specs = (
        P(AXES, None),
        P("items", None),
        P(AXES, None),
        P(AXES, None),
        P(AXES),
        P(AXES, None, None, None),
        P(AXES, None, None, None),
    )
    out_specs = (P(AXES, None), P(AXES, None))
    return jax.shard_map(body, mesh=mesh, in_specs=in_specs, out_specs=out_specs, check_vma=False)
```

time: 315 us -> 48.6 us (0.15)
  waiting for transfers between devices: 140 us -> 8.55 us
  matrix products: 127 us -> 0 us
  between operations: 14.8 us -> 1.4 us
  other arithmetic: 13 us -> 0.73 us
  Pallas kernels: 0 us -> 10.9 us
  starting transfers between devices: 0.04 us -> 9.03 us
    reduce_scatter x1 -> x0, waiting for transfers between devices: 140 us -> none  [body(): lax.psum_scatter(item_acc.reshape(-1, rank_width), ('users', 'items'), sc...]
    dot_general x105 -> x0, matrix products: 127 us -> none  [the longest x30 52.5 us: add_tiles(): jnp.einsum('gb,gur->bur', selector, terms, precision=lax.Precision.HIGHES...]
    pallas_call x0 -> x2, Pallas kernels: none -> 10.9 us  [the longest x1 6.12 us: body(): pl.pallas_call(functools.partial(item_kernel, unroll, device_total, group...]
    lt x15 -> x0, other arithmetic: 9.79 us -> none  [group_terms(): live_rows = first_slot + slot_offsets < live_count]
    ppermute x0 -> x7, starting transfers between devices: none -> 9.03 us  [permute(): lax.ppermute(array, AXES, [(index, index ^ mask) for index in range(devic...]
    ppermute x0 -> x7, waiting for transfers between devices: none -> 8.55 us  [permute(): lax.ppermute(array, AXES, [(index, index ^ mask) for index in range(devic...]
    unnamed x12 -> x14, local copies, waits for them, and re-layouts: 2.99 us -> 6.91 us
  transfers between devices with their start and end apart: 1 -> 7, of which waited for: 1 -> 5; matrix products, arithmetic and copies ran while one was open for 1% -> 0% of each run, Pallas kernels for 0% -> 10%
where the time goes in v1:
time: 48.6 us; the launch traced here: 48.1 us
  Pallas kernels  10.9 us (22%)
  starting transfers between devices  9.03 us (19%)
  blocking collectives  8.86 us (18%)
  local copies, waits for them, and re-layouts  8.57 us (18%)
  waiting for transfers between devices  8.55 us (18%)
  between operations  1.4 us (3%)
  other arithmetic  0.73 us (2%)
    ppermute x7, starting transfers between devices, permute(): lax.ppermute(array, AXES, [(index, index ^ mask) for index in range(devic...  9.03 us
    all_gather x1, blocking collectives, body(): item_whole = lax.all_gather(item_factors, 'items', axis=0, tiled=True)  8.86 us
    ppermute x7, waiting for transfers between devices, permute(): lax.ppermute(array, AXES, [(index, index ^ mask) for index in range(devic...  8.55 us
    unnamed x14, local copies, waits for them, and re-layouts  6.91 us
    pallas_call x1, Pallas kernels, body(): pl.pallas_call(functools.partial(item_kernel, unroll, device_total, group...  6.12 us
    pallas_call x1, Pallas kernels, body(): pl.pallas_call(functools.partial(user_kernel, unroll), out_shape=jax.Shap...  4.8 us
    reshape x1, local copies, waits for them, and re-layouts, body(): turned = user_factors.reshape(-1, block, rank).swapaxes(1, 2)  1.62 us
  transfers between devices with their start and end apart: 7, of which 5 were waited for; matrix products, arithmetic and copies ran while one was open for 0% of the time, Pallas kernels for 10%

profile of v1, /device:TPU:0, one launch (start us, length us, event | category | flops | bytes accessed | tf_op | source)
XLA Modules:
  0.0 48.1 jit_solution(7929488234498047216)
XLA Ops:
  0.6 8.9 %all_gather.3.item_ref = bf16[1024,256]{1,0:T(8,128)(2,1)S(1)} all-gather(bf16[256,256]{1,0:T(8,128)(2,1)} %param.8), channel_id=1, replica_groups=mesh['users'=8,'items'=4] {'items'}, dimensions={0}, use_global_device_ids=true | all-gather | bytes 655360 | tf_op jit(solution)/shard_map/all_gather | solution.py:122
  10.2 1.6 %copy.9 = bf16[16,128,256]{1,2,0:T(8,128)(2,1)S(1)} copy(bf16[16,128,256]{2,1,0:T(8,128)(2,1)} %bitcast.3) | data formatting | bytes 2097152 | tf_op jit(solution)/shard_map/reshape | solution.py:124
  11.8 0.0 copy-start
  11.8 1.2 %copy-done = bf16[2048,256]{1,0:T(8,128)(2,1)S(1)} copy-done((bf16[2048,256]{1,0:T(8,128)(2,1)S(1)}, bf16[2048,256]{1,0:T(8,128)(2,1)}, u32[]{:S(2)}) %copy-start) | copy-done | bytes 1048600
  13.0 0.0 copy-start.2
  13.0 2.2 %copy-done.2 = bf16[1,128,128,128]{3,2,1,0:T(8,128)(2,1)S(1)} copy-done((bf16[1,128,128,128]{3,2,1,0:T(8,128)(2,1)S(1)}, bf16[1,128,128,128]{3,2,1,0:T(8,128)(2,1)}, u32[]{:S(2)}) %copy-start.2) | copy-done | bytes 4194328
  15.2 0.0 copy-start.3
  15.2 2.2 %copy-done.3 = bf16[1,128,128,128]{3,2,1,0:T(8,128)(2,1)S(1)} copy-done((bf16[1,128,128,128]{3,2,1,0:T(8,128)(2,1)S(1)}, bf16[1,128,128,128]{3,2,1,0:T(8,128)(2,1)}, u32[]{:S(2)}) %copy-start.3) | copy-done | bytes 4194328
  17.4 0.0 copy-start.4
  17.4 0.7 %copy-done.4 = s32[1,128]{1,0:T(1,128)S(1)} copy-done((s32[1,128]{1,0:T(1,128)S(1)}, s32[1,128]{1,0:T(1,128)}, u32[]{:S(2)}) %copy-start.4) | copy-done | bytes 536
  18.0 0.0 copy-start.6
  18.1 0.7 %copy-done.6 = s32[1,128]{1,0:T(1,128)S(1)} copy-done((s32[1,128]{1,0:T(1,128)S(1)}, s32[1,128]{1,0:T(1,128)}, u32[]{:S(2)}) %copy-start.6) | copy-done | bytes 536
  18.7 0.0 copy-start.1
  18.7 0.0 copy-start.5
  18.7 6.1 %item_sums.1 = (f32[512,256]{1,0:T(8,128)S(1)}, f32[512,256]{1,0:T(8,128)S(1)}, bf16[128,128,128]{2,1,0:T(8,128)(2,1)S(1)}) custom-call(s32[1]{0:T(128)S(6)} %copy.10.count_ref, s32[1]{0:T(128)} %bitcast.place_ref, s32[1,128]{1,0:T(1,128)S(1)} %copy-done.4, s32[1,128]{1,0:T(1,128)S(1)} %copy-done.6, bf16[2048,256]{1,0:T(8,128)(2,1)S(1)} %copy-done, ...), custom_call_target="tpu_custom_call" | custom-call | tf_op jit(solution)/shard_map/item_sums/pallas_call | solution.py:127
  24.8 0.1 collective-permute-start
  24.9 1.9 %collective-permute-done = f32[512,256]{1,0:T(8,128)S(1)} collective-permute-done((f32[512,256]{1,0:T(8,128)S(1)}, f32[512,256]{1,0:T(8,128)S(1)}, u32[]{:S(2)}, u32[]{:S(2)}) %collective-permute-start) | collective-permute-done | bytes 524320 | tf_op jit(solution)/shard_map/ppermute | solution.py:148
  26.8 0.1 add.47
  26.9 2.6 %collective-permute-start.1 = (f32[128,256]{1,0:T(8,128)S(1)}, f32[128,256]{1,0:T(8,128)S(1)}, u32[]{:S(2)}, u32[]{:S(2)}) collective-permute-start(f32[128,256]{1,0:T(8,128)S(1)} %get-tuple-element.8), channel_id=1, source_target_pairs={{0,2},{1,3},{2,0},{3,1},{4,6},{5,7},{6,4},{7,5},{8,10},{9,11},{10,... | collective-permute-start | bytes 393224 | tf_op jit(solution)/shard_map/ppermute | solution.py:148
  29.6 1.5 %collective-permute-start.2 = (f32[128,256]{1,0:T(8,128)S(1)}, f32[128,256]{1,0:T(8,128)S(1)}, u32[]{:S(2)}, u32[]{:S(2)}) collective-permute-start(f32[128,256]{1,0:T(8,128)S(1)} %get-tuple-element.10), channel_id=1, source_target_pairs={{0,4},{1,5},{2,6},{3,7},{4,0},{5,1},{6,2},{7,3},{8,12},{9,13},{10,... | collective-permute-start | bytes 393224 | tf_op jit(solution)/shard_map/ppermute | solution.py:148
  31.1 0.4 collective-permute-start.3
  31.4 1.9 %collective-permute-done.1 = f32[128,256]{1,0:T(8,128)S(1)} collective-permute-done((f32[128,256]{1,0:T(8,128)S(1)}, f32[128,256]{1,0:T(8,128)S(1)}, u32[]{:S(2)}, u32[]{:S(2)}) %collective-permute-start.1) | collective-permute-done | bytes 131104 | tf_op jit(solution)/shard_map/ppermute | solution.py:148
  33.4 2.5 %collective-permute-done.2 = f32[128,256]{1,0:T(8,128)S(1)} collective-permute-done((f32[128,256]{1,0:T(8,128)S(1)}, f32[128,256]{1,0:T(8,128)S(1)}, u32[]{:S(2)}, u32[]{:S(2)}) %collective-permute-start.2) | collective-permute-done | bytes 131104 | tf_op jit(solution)/shard_map/ppermute | solution.py:148
  35.9 2.1 %collective-permute-done.3 = f32[128,256]{1,0:T(8,128)S(1)} collective-permute-done((f32[128,256]{1,0:T(8,128)S(1)}, f32[128,256]{1,0:T(8,128)S(1)}, u32[]{:S(2)}, u32[]{:S(2)}) %collective-permute-start.3) | collective-permute-done | bytes 131104 | tf_op jit(solution)/shard_map/ppermute | solution.py:148
  38.0 0.4 collective-permute-start.4
  38.4 3.3 %collective-permute-start.5 = (f32[32,256]{1,0:T(8,128)S(1)}, f32[32,256]{1,0:T(8,128)S(1)}, u32[]{:S(2)}, u32[]{:S(2)}) collective-permute-start(f32[32,256]{1,0:T(8,128)S(1)} %get-tuple-element.13), channel_id=1, source_target_pairs={{0,16},{1,17},{2,18},{3,19},{4,20},{5,21},{6,22},{7,23},{8,24},{9,... | collective-permute-start | bytes 98312 | tf_op jit(solution)/shard_map/ppermute | solution.py:148
  41.7 0.8 %collective-permute-start.6 = (f32[32,256]{1,0:T(8,128)S(1)}, f32[32,256]{1,0:T(8,128)S(1)}, u32[]{:S(2)}, u32[]{:S(2)}) collective-permute-start(f32[32,256]{1,0:T(8,128)S(1)} %get-tuple-element.12), channel_id=1, source_target_pairs={{0,24},{1,25},{2,26},{3,27},{4,28},{5,29},{6,30},{7,31},{8,16},{9,... | collective-permute-start | bytes 98312 | tf_op jit(solution)/shard_map/ppermute | solution.py:148
  42.5 0.0 copy-done.1
  42.5 0.0 copy-done.5
  42.5 4.8 %user_sums.1 = f32[2048,256]{1,0:T(8,128)} custom-call(s32[1]{0:T(128)S(6)} %copy.10.count_ref, s32[1,128]{1,0:T(1,128)S(1)} %copy-done.5, s32[1,128]{1,0:T(1,128)S(1)} %copy-done.6, bf16[2048,256]{1,0:T(8,128)(2,1)S(1)} %copy-done.1, bf16[1024,256]{1,0:T(8,128)(2,1)S(1)} %all_gather.3.item_ref, bf16[128,128,128]{2,1,0:T(8,128)(2,1)S(1)} %get-tuple-element.5.weighted_ref), custom_call_target="tpu_custom_call" | custom-call | flops 1073741824 | bytes 8388608 | tf_op jit(solution)/shard_map/user_sums/pallas_call | solution.py:136
  47.3 0.0 collective-permute-done.4
  47.3 0.0 collective-permute-done.5
  47.3 0.1 collective-permute-done.6
  47.4 0.6 %fusion.5 = f32[32,256]{1,0:T(8,128)} fusion(f32[32,256]{1,0:T(8,128)S(1)} %collective-permute-done.6, f32[32,256]{1,0:T(8,128)S(1)} %collective-permute-done.5, f32[32,256]{1,0:T(8,128)S(1)} %collective-permute-done.4, f32[128,256]{1,0:T(8,128)S(1)} %fusion.1, bf16[1024,256]{1,0:T(8,128)(2,1)S(1)} %all_gather.3.item_ref, s32[]{:T(128)S(6)} %select_n.3), kind=kLoop, calls=%fused_computation.7 | loop fusion | flops 57344 | bytes 180228 | tf_op jit(solution)/shard_map/add | solution.py:163
  (3 shorter events, 0.1 us)
Async XLA Ops:
  11.8 1.2 %copy-start = (bf16[2048,256]{1,0:T(8,128)(2,1)S(1)}, bf16[2048,256]{1,0:T(8,128)(2,1)}, u32[]{:S(2)}) copy-start(bf16[2048,256]{1,0:T(8,128)(2,1)} %user_ref.3) | copy-start | bytes 3145732
  13.0 2.2 %copy-start.2 = (bf16[1,128,128,128]{3,2,1,0:T(8,128)(2,1)S(1)}, bf16[1,128,128,128]{3,2,1,0:T(8,128)(2,1)}, u32[]{:S(2)}) copy-start(bf16[1,128,128,128]{3,2,1,0:T(8,128)(2,1)} %rating_ref.1) | copy-start | bytes 12582916
  15.2 2.2 %copy-start.3 = (bf16[1,128,128,128]{3,2,1,0:T(8,128)(2,1)S(1)}, bf16[1,128,128,128]{3,2,1,0:T(8,128)(2,1)}, u32[]{:S(2)}) copy-start(bf16[1,128,128,128]{3,2,1,0:T(8,128)(2,1)} %weight_ref.1) | copy-start | bytes 12582916
  17.4 0.7 %copy-start.4 = (s32[1,128]{1,0:T(1,128)S(1)}, s32[1,128]{1,0:T(1,128)}, u32[]{:S(2)}) copy-start(s32[1,128]{1,0:T(1,128)} %user_id_ref.3) | copy-start | bytes 1540
  18.0 0.7 %copy-start.6 = (s32[1,128]{1,0:T(1,128)S(1)}, s32[1,128]{1,0:T(1,128)}, u32[]{:S(2)}) copy-start(s32[1,128]{1,0:T(1,128)} %item_id_ref.3) | copy-start | bytes 1540
  18.7 23.8 %copy-start.1 = (bf16[2048,256]{1,0:T(8,128)(2,1)S(1)}, bf16[2048,256]{1,0:T(8,128)(2,1)}, u32[]{:S(2)}) copy-start(bf16[2048,256]{1,0:T(8,128)(2,1)} %user_ref.3) | copy-start | bytes 3145732
  18.7 23.8 %copy-start.5 = (s32[1,128]{1,0:T(1,128)S(1)}, s32[1,128]{1,0:T(1,128)}, u32[]{:S(2)}) copy-start(s32[1,128]{1,0:T(1,128)} %user_id_ref.3) | copy-start | bytes 1540
  24.8 2.0 %collective-permute-start = (f32[512,256]{1,0:T(8,128)S(1)}, f32[512,256]{1,0:T(8,128)S(1)}, u32[]{:S(2)}, u32[]{:S(2)}) collective-permute-start(f32[512,256]{1,0:T(8,128)S(1)} %get-tuple-element.7), channel_id=1, source_target_pairs={{0,1},{1,0},{2,3},{3,2},{4,5},{5,4},{6,7},{7,6},{8,9},{9,8},{10,11... | collective-permute-start | bytes 1572872 | tf_op jit(solution)/shard_map/ppermute | solution.py:148
  26.9 6.4 %collective-permute-start.1 = (f32[128,256]{1,0:T(8,128)S(1)}, f32[128,256]{1,0:T(8,128)S(1)}, u32[]{:S(2)}, u32[]{:S(2)}) collective-permute-start(f32[128,256]{1,0:T(8,128)S(1)} %get-tuple-element.8), channel_id=1, source_target_pairs={{0,2},{1,3},{2,0},{3,1},{4,6},{5,7},{6,4},{7,5},{8,10},{9,11},{10,... | collective-permute-start | bytes 393224 | tf_op jit(solution)/shard_map/ppermute | solution.py:148
  29.6 6.3 %collective-permute-start.2 = (f32[128,256]{1,0:T(8,128)S(1)}, f32[128,256]{1,0:T(8,128)S(1)}, u32[]{:S(2)}, u32[]{:S(2)}) collective-permute-start(f32[128,256]{1,0:T(8,128)S(1)} %get-tuple-element.10), channel_id=1, source_target_pairs={{0,4},{1,5},{2,6},{3,7},{4,0},{5,1},{6,2},{7,3},{8,12},{9,13},{10,... | collective-permute-start | bytes 393224 | tf_op jit(solution)/shard_map/ppermute | solution.py:148
  31.1 6.9 %collective-permute-start.3 = (f32[128,256]{1,0:T(8,128)S(1)}, f32[128,256]{1,0:T(8,128)S(1)}, u32[]{:S(2)}, u32[]{:S(2)}) collective-permute-start(f32[128,256]{1,0:T(8,128)S(1)} %get-tuple-element.9), channel_id=1, source_target_pairs={{0,6},{1,7},{2,4},{3,5},{4,2},{5,3},{6,0},{7,1},{8,14},{9,15},{10,... | collective-permute-start | bytes 393224 | tf_op jit(solution)/shard_map/ppermute | solution.py:148
  38.0 9.3 %collective-permute-start.4 = (f32[32,256]{1,0:T(8,128)S(1)}, f32[32,256]{1,0:T(8,128)S(1)}, u32[]{:S(2)}, u32[]{:S(2)}) collective-permute-start(f32[32,256]{1,0:T(8,128)S(1)} %get-tuple-element.11), channel_id=1, source_target_pairs={{0,8},{1,9},{2,10},{3,11},{4,12},{5,13},{6,14},{7,15},{8,0},{9,1},... | collective-permute-start | bytes 98312 | tf_op jit(solution)/shard_map/ppermute | solution.py:148
  38.4 8.9 %collective-permute-start.5 = (f32[32,256]{1,0:T(8,128)S(1)}, f32[32,256]{1,0:T(8,128)S(1)}, u32[]{:S(2)}, u32[]{:S(2)}) collective-permute-start(f32[32,256]{1,0:T(8,128)S(1)} %get-tuple-element.13), channel_id=1, source_target_pairs={{0,16},{1,17},{2,18},{3,19},{4,20},{5,21},{6,22},{7,23},{8,24},{9,... | collective-permute-start | bytes 98312 | tf_op jit(solution)/shard_map/ppermute | solution.py:148
  41.7 5.7 %collective-permute-start.6 = (f32[32,256]{1,0:T(8,128)S(1)}, f32[32,256]{1,0:T(8,128)S(1)}, u32[]{:S(2)}, u32[]{:S(2)}) collective-permute-start(f32[32,256]{1,0:T(8,128)S(1)} %get-tuple-element.12), channel_id=1, source_target_pairs={{0,24},{1,25},{2,26},{3,27},{4,28},{5,29},{6,30},{7,31},{8,16},{9,... | collective-permute-start | bytes 98312 | tf_op jit(solution)/shard_map/ppermute | solution.py:148

commit v2 on v1

v2 whole, which is shorter than its diff:
```python
import functools

import jax
import jax.numpy as jnp
from jax import lax
from jax.experimental import pallas as pl
from jax.experimental.pallas import tpu as pltpu
from jax.sharding import PartitionSpec as P

grad_scale = 0.015625
decay_rate = 0.05
AXES = ("users", "items")
VMEM = pl.BlockSpec(memory_space=pltpu.VMEM)
SMEM = pl.BlockSpec(memory_space=pltpu.SMEM)
HBM = pl.BlockSpec(memory_space=pltpu.HBM)


def phases_of(device_total):
    bit_total = device_total.bit_length() - 1
    groups = [[0]]
    for bit in range(1, bit_total, 2):
        groups.append(list(range(bit, min(bit + 2, bit_total))))
    return groups


def place_of(index, groups):
    place = 0
    for group in groups:
        for bit in reversed(group):
            place = place * 2 + ((index >> bit) & 1)
    return place


def add_slots(unroll, first_turn, turn_total, slot_of, valid_total, user_id_ref, item_id_ref, item_row_of, user_ref,
              turned_ref, item_ref, rating_ref, weight_ref, total, before, after):
    block = rating_ref.shape[1]

    def turn(index, carry):
        base = index * unroll
        carry = before(base, carry)
        slots = [slot_of(base + step) for step in range(unroll)]
        predicted = []
        for slot in slots:
            user_row = pl.multiple_of(user_id_ref[0, slot] * block, block)
            item_row = pl.multiple_of(item_row_of(item_id_ref[0, slot]), block)
            predicted.append(lax.dot_general(
                user_ref[pl.ds(user_row, block), :], item_ref[pl.ds(item_row, block), :],
                (((1,), (1,)), ((), ())), preferred_element_type=jnp.float32))
        tiles = []
        for step, slot in enumerate(slots):
            weighted = weight_ref[slot].astype(jnp.float32) * (
                predicted[step] - rating_ref[slot].astype(jnp.float32))
            tiles.append(jnp.where(base + step < valid_total, weighted, 0.0).astype(jnp.bfloat16))
        terms = [jnp.dot(turned_ref[user_id_ref[0, slot]], tile, preferred_element_type=jnp.float32)
                 for slot, tile in zip(slots, tiles)]
        after(base, slots, tiles)
        for slot, term in zip(slots, terms):
            total[item_id_ref[0, slot]] += term
        return carry

    return lax.fori_loop(first_turn, turn_total, turn, 0)


def near_kernel(unroll, count_ref, place_ref, user_id_ref, item_id_ref, user_ref, own_ref, pair_ref, rating_ref,
                weight_ref, total, user_total, turned_ref, factor_ref, held_rating_ref, held_weight_ref, order_ref,
                item_ref, factor_sem, rating_sems, weight_sems):
    live = count_ref[0]
    item_mask = place_ref[1]
    slots = held_rating_ref.shape[0]
    block = held_rating_ref.shape[1]
    chunks = (live + unroll - 1) // unroll
    panel_rows = own_ref.shape[0]
    near_blocks = 2 * panel_rows // block

    def copies(index):
        part = pl.ds(index * unroll, unroll)
        return (
            pltpu.make_async_copy(rating_ref.at[0, part], held_rating_ref.at[part], rating_sems.at[index]),
            pltpu.make_async_copy(weight_ref.at[0, part], held_weight_ref.at[part], weight_sems.at[index]),
        )

    factor_copy = pltpu.make_async_copy(user_ref, factor_ref, factor_sem)
    factor_copy.start()
    for index in range(slots // unroll):
        @pl.when(index < chunks)
        def _():
            for copy in copies(index):
                copy.start()

    def sort(slot, near_total):
        near = (item_id_ref[0, slot] ^ item_mask) < near_blocks
        order_ref[jnp.where(near, near_total, slots - 1 - slot + near_total)] = slot
        return near_total + near.astype(jnp.int32)

    near_total = lax.fori_loop(0, live, sort, 0)
    order_ref[slots] = near_total
    item_ref[:panel_rows, :] = own_ref[...]
    item_ref[panel_rows:, :] = pair_ref[...]
    total[...] = jnp.zeros_like(total)
    user_total[...] = jnp.zeros_like(user_total)
    factor_copy.wait()
    for index in range(turned_ref.shape[0]):
        turned_ref[index] = factor_ref[index * block:(index + 1) * block, :].T

    def wait(index, carry):
        for copy in copies(index):
            copy.wait()
        return carry

    def item_row_of(item):
        return (item ^ item_mask) % near_blocks * block

    def slot_of(position):
        return jnp.where(position < near_total, order_ref[position], 0)

    def before(base, waited):
        needed = order_ref[jnp.minimum(base + unroll, near_total) - 1] // unroll + 1
        lax.fori_loop(waited, needed, wait, 0)
        return needed

    def after(base, slot_list, tiles):
        terms = []
        for slot, tile in zip(slot_list, tiles):
            item_row = pl.multiple_of(item_row_of(item_id_ref[0, slot]), block)
            terms.append(jnp.dot(tile, item_ref[pl.ds(item_row, block), :], preferred_element_type=jnp.float32))
        for slot, term in zip(slot_list, terms):
            user_row = pl.multiple_of(user_id_ref[0, slot] * block, block)
            user_total[pl.ds(user_row, block), :] += term

    waited = add_slots(unroll, 0, (near_total + unroll - 1) // unroll, slot_of, near_total, user_id_ref, item_id_ref,
                       item_row_of, factor_ref, turned_ref, item_ref, held_rating_ref, held_weight_ref, total, before,
                       after)
    lax.fori_loop(waited, chunks, wait, 0)


def far_kernel(unroll, owner_total, groups, count_ref, place_ref, user_id_ref, item_id_ref, order_ref, user_ref,
               turned_ref, near_ref, rating_ref, weight_ref, *refs):
    panel_refs, (keep_ref, send_ref, weighted_ref, item_ref, total) = refs[:-5], refs[-5:]
    slots = rating_ref.shape[0]
    block = rating_ref.shape[1]
    item_mask = place_ref[1]
    far_total = count_ref[0] - order_ref[slots]
    row = 0
    for panel_ref in panel_refs:
        item_ref[row:row + panel_ref.shape[0], :] = panel_ref[...]
        row += panel_ref.shape[0]
    total[...] = near_ref[...]

    def slot_of(position):
        return jnp.where(position < far_total, order_ref[slots - 1 - position], 0)

    def after(base, slot_list, tiles):
        for step, tile in enumerate(tiles):
            weighted_ref[base + step] = tile

    add_slots(unroll, 0, (far_total + unroll - 1) // unroll, slot_of, far_total, user_id_ref, item_id_ref,
              lambda item: (item ^ item_mask) * block, user_ref, turned_ref, item_ref, rating_ref, weight_ref, total,
              lambda base, carry: carry, after)
    own_place = place_ref[0]
    owned = keep_ref.shape[0] * 2 // owner_total
    half = owner_total // 2
    per_block = block // owned
    for item in range(total.shape[0]):
        rows = total[item].T
        for part in range(per_block):
            place = own_place ^ place_of(item * per_block + part, groups)
            piece = rows[part * owned:(part + 1) * owned]
            row = pl.multiple_of((place % half) * owned, owned)

            @pl.when(place < half)
            def _():
                keep_ref[pl.ds(row, owned), :] = piece

            @pl.when(place >= half)
            def _():
                send_ref[pl.ds(row, owned), :] = piece


def user_kernel(unroll, count_ref, place_ref, user_id_ref, item_id_ref, order_ref, near_ref, item_ref, user_ref,
                weighted_ref, grad_ref, total_ref, sems):
    slots = weighted_ref.shape[0]
    block = weighted_ref.shape[1]
    item_mask = place_ref[1]
    far_total = count_ref[0] - order_ref[slots]
    total_ref[...] = near_ref[...]

    def turn(index, carry):
        base = index * unroll
        chosen = [jnp.where(base + step < far_total, order_ref[slots - 1 - base - step], 0) for step in range(unroll)]
        terms = []
        for step, slot in enumerate(chosen):
            item_row = pl.multiple_of((item_id_ref[0, slot] ^ item_mask) * block, block)
            terms.append(jnp.dot(weighted_ref[base + step], item_ref[pl.ds(item_row, block), :],
                                 preferred_element_type=jnp.float32))
        for slot, term in zip(chosen, terms):
            user_row = pl.multiple_of(user_id_ref[0, slot] * block, block)
            total_ref[pl.ds(user_row, block), :] += term
        return carry

    lax.fori_loop(0, (far_total + unroll - 1) // unroll, turn, 0)

    def writeback(index):
        rows = pl.ds(index * block, block)
        return pltpu.make_async_copy(total_ref.at[rows], grad_ref.at[rows], sems.at[index])

    blocks = total_ref.shape[0] // block
    for index in range(blocks):
        rows = pl.ds(index * block, block)
        total_ref[rows, :] = total_ref[rows, :] * grad_scale + decay_rate * user_ref[rows, :].astype(jnp.float32)
        writeback(index).start()
    for index in range(blocks):
        writeback(index).wait()


def body(user_factors, item_factors, block_user, block_item, counts, ratings, weights):
    rank = user_factors.shape[1]
    slots, block = ratings.shape[1], ratings.shape[2]
    user_rows = user_factors.shape[0]
    panel_rows = item_factors.shape[0]
    panel_total = lax.axis_size("items")
    device_total = lax.axis_size("users") * panel_total
    panel_index = lax.axis_index("items")
    me = lax.axis_index("users") * panel_total + panel_index
    groups = phases_of(device_total)
    unroll = 16
    item_rows = panel_rows * panel_total

    def permute(array, mask):
        return lax.ppermute(array, AXES, [(index, index ^ mask) for index in range(device_total)])

    def estimate(micros):
        return pl.CostEstimate(flops=0, bytes_accessed=int(3e6 * micros), transcendentals=0)

    panels = [item_factors] + [permute(item_factors, mask) for mask in range(1, panel_total)]
    places = jnp.stack([place_of(me, groups), panel_index * (panel_rows // block)]).astype(jnp.int32)
    held = jax.ShapeDtypeStruct((slots, block, block), jnp.bfloat16)
    sums_shape = jax.ShapeDtypeStruct((item_rows // block, rank, block), jnp.float32)
    user_shape = jax.ShapeDtypeStruct((user_rows, rank), jnp.float32)
    near_sums, near_users, turned, factors, held_ratings, held_weights, order = pl.pallas_call(
        functools.partial(near_kernel, unroll),
        out_shape=(
            sums_shape,
            user_shape,
            jax.ShapeDtypeStruct((user_rows // block, rank, block), jnp.bfloat16),
            jax.ShapeDtypeStruct((user_rows, rank), jnp.bfloat16),
            held,
            held,
            jax.ShapeDtypeStruct((slots + 8,), jnp.int32),
        ),
        in_specs=[SMEM] * 4 + [HBM] + [VMEM] * 2 + [HBM] * 2,
        out_specs=(VMEM,) * 6 + (SMEM,),
        scratch_shapes=[pltpu.VMEM((2 * panel_rows, rank), jnp.bfloat16), pltpu.SemaphoreType.DMA]
        + [pltpu.SemaphoreType.DMA((slots // unroll,))] * 2,
        compiler_params=pltpu.CompilerParams(vmem_limit_bytes=37 << 20),
        cost_estimate=estimate(8),
        name="near_sums",
    )(counts, places, block_user, block_item, user_factors, panels[0], panels[1], ratings, weights)

    half_shape = jax.ShapeDtypeStruct((item_rows // 2, rank), jnp.float32)
    keep, send, weighted, item_whole = pl.pallas_call(
        functools.partial(far_kernel, unroll, device_total, groups),
        out_shape=(half_shape, half_shape, held, jax.ShapeDtypeStruct((item_rows, rank), jnp.bfloat16)),
        in_specs=[SMEM] * 5 + [VMEM] * (5 + panel_total),
        out_specs=(VMEM,) * 4,
        scratch_shapes=[pltpu.VMEM(sums_shape.shape, jnp.float32)],
        compiler_params=pltpu.CompilerParams(vmem_limit_bytes=12 << 20),
        cost_estimate=estimate(5),

        name="far_sums",
    )(counts, places, block_user, block_item, order, factors, turned, near_sums, held_ratings, held_weights, *panels)

    partial = keep + permute(send, 1)
    user_grad = pl.pallas_call(
        functools.partial(user_kernel, unroll),
        out_shape=user_shape,
        in_specs=[SMEM] * 5 + [VMEM] * 4,
        out_specs=HBM,
        scratch_shapes=[pltpu.VMEM(user_shape.shape, user_shape.dtype),
                        pltpu.SemaphoreType.DMA((user_rows // block,))],
        compiler_params=pltpu.CompilerParams(vmem_limit_bytes=12 << 20),
        cost_estimate=estimate(3),
        name="user_sums",
    )(counts, places, block_user, block_item, order, near_users, item_whole, factors, weighted)
    for group in groups[1:]:
        ways = 1 << len(group)
        parts = partial.reshape(ways, -1, rank)
        partial = parts[0]
        for way in reversed(range(1, ways)):
            mask = sum(((way >> index) & 1) << bit for index, bit in enumerate(group))
            partial = partial + permute(parts[way], mask)
    owned_rows = partial.shape[0]
    own_row = (me * owned_rows) ^ (panel_index * panel_rows)
    own_factors = lax.dynamic_slice_in_dim(item_whole, own_row, owned_rows, 0)
    item_grad = partial * grad_scale + decay_rate * own_factors.astype(jnp.float32)
    return (user_grad, item_grad)


def solution(mesh):
    in_specs = (
        P(AXES, None),
        P("items", None),
        P(AXES, None),
        P(AXES, None),
        P(AXES),
        P(AXES, None, None, None),
        P(AXES, None, None, None),
    )
    out_specs = (P(AXES, None), P(AXES, None))
    return jax.shard_map(body, mesh=mesh, in_specs=in_specs, out_specs=out_specs, check_vma=False)
```

time: 48.6 us -> 46.6 us (0.959)
  blocking collectives: 8.86 us -> 0 us
  starting transfers between devices: 9.03 us -> 17.6 us
  Pallas kernels: 10.9 us -> 8.77 us
  local copies, waits for them, and re-layouts: 8.57 us -> 9.44 us
    all_gather x1 -> x0, blocking collectives: 8.86 us -> none  [body(): item_whole = lax.all_gather(item_factors, 'items', axis=0, tiled=True)]
    ppermute x7 -> x10, starting transfers between devices: 9.03 us -> 17.6 us  [permute(): lax.ppermute(array, AXES, [(index, index ^ mask) for index in range(devic...]
    unnamed x14 -> x20, local copies, waits for them, and re-layouts: 6.91 us -> 9.4 us
    pallas_call x2 -> x3, Pallas kernels: 10.9 us -> 8.77 us  [the longest x1 3.64 us: body(): pl.pallas_call(functools.partial(near_kernel, unroll), out_shape=(sums_sh...]
    reshape x1 -> x0, local copies, waits for them, and re-layouts: 1.62 us -> none  [body(): turned = user_factors.reshape(-1, block, rank).swapaxes(1, 2)]
    ppermute x7 -> x10, waiting for transfers between devices: 8.55 us -> 8.14 us  [permute(): lax.ppermute(array, AXES, [(index, index ^ mask) for index in range(devic...]
  transfers between devices with their start and end apart: 7 -> 10, of which waited for: 5 -> 4; matrix products, arithmetic and copies ran while one was open for 0% -> 0% of each run, Pallas kernels for 10% -> 14%
where the time goes in v2:
time: 46.6 us; the launch traced here: 46.2 us
  starting transfers between devices  17.6 us (38%)
  local copies, waits for them, and re-layouts  9.44 us (20%)
  Pallas kernels  8.77 us (19%)
  waiting for transfers between devices  8.14 us (17%)
  between operations  1.42 us (3%)
  other arithmetic  0.82 us (2%)
    ppermute x10, starting transfers between devices, permute(): lax.ppermute(array, AXES, [(index, index ^ mask) for index in range(devic...  17.6 us
    unnamed x20, local copies, waits for them, and re-layouts  9.4 us
    ppermute x10, waiting for transfers between devices, permute(): lax.ppermute(array, AXES, [(index, index ^ mask) for index in range(devic...  8.14 us
    pallas_call x1, Pallas kernels, body(): pl.pallas_call(functools.partial(near_kernel, unroll), out_shape=(sums_sh...  3.64 us
    pallas_call x1, Pallas kernels, body(): pl.pallas_call(functools.partial(user_kernel, unroll), out_shape=user_sha...  2.61 us
    pallas_call x1, Pallas kernels, body(): pl.pallas_call(functools.partial(far_kernel, unroll, device_total, groups...  2.52 us
  transfers between devices with their start and end apart: 10, of which 4 were waited for; matrix products, arithmetic and copies ran while one was open for 0% of the time, Pallas kernels for 14%

profile of v2, /device:TPU:0, one launch (start us, length us, event | category | flops | bytes accessed | tf_op | source)
XLA Modules:
  0.0 46.2 jit_solution(11285344693457842378)
XLA Ops:
  0.6 0.5 %collective-permute-start = (bf16[256,256]{1,0:T(8,128)(2,1)}, bf16[256,256]{1,0:T(8,128)(2,1)S(1)}, u32[]{:S(2)}, u32[]{:S(2)}) collective-permute-start(bf16[256,256]{1,0:T(8,128)(2,1)} %refs_0_.1), channel_id=1, source_target_pairs={{0,1},{1,0},{2,3},{3,2},{4,5},{5,4},{6,7},{7,6},{8,9},{9,8},{10,11... | collective-permute-start | bytes 393224 | tf_op jit(solution)/shard_map/ppermute | solution.py:229
  1.1 2.6 %collective-permute-start.1 = (bf16[256,256]{1,0:T(8,128)(2,1)}, bf16[256,256]{1,0:T(8,128)(2,1)S(1)}, u32[]{:S(2)}, u32[]{:S(2)}) collective-permute-start(bf16[256,256]{1,0:T(8,128)(2,1)} %refs_0_.1), channel_id=1, source_target_pairs={{0,2},{1,3},{2,0},{3,1},{4,6},{5,7},{6,4},{7,5},{8,10},{9,11},{10,... | collective-permute-start | bytes 393224 | tf_op jit(solution)/shard_map/ppermute | solution.py:229
  3.7 0.1 collective-permute-start.2
  4.5 0.1 pad_add_fusion.place_ref
  4.5 0.0 collective-permute-done.pair_ref.refs_1_
  4.5 0.0 copy-start.2
  4.5 1.2 %copy-done.2 = bf16[2048,256]{1,0:T(8,128)(2,1)S(1)} copy-done((bf16[2048,256]{1,0:T(8,128)(2,1)S(1)}, bf16[2048,256]{1,0:T(8,128)(2,1)}, u32[]{:S(2)}) %copy-start.2) | copy-done | bytes 1048600
  5.8 0.0 copy-start.5
  5.8 0.9 %copy-done.5 = bf16[256,256]{1,0:T(8,128)(2,1)S(1)} copy-done((bf16[256,256]{1,0:T(8,128)(2,1)S(1)}, bf16[256,256]{1,0:T(8,128)(2,1)}, u32[]{:S(2)}) %copy-start.5) | copy-done | bytes 131096
  6.7 0.0 copy-start.6
  6.7 0.7 %copy-done.6 = s32[1,128]{1,0:T(1,128)S(1)} copy-done((s32[1,128]{1,0:T(1,128)S(1)}, s32[1,128]{1,0:T(1,128)}, u32[]{:S(2)}) %copy-start.6) | copy-done | bytes 536
  7.3 0.0 copy-start.8
  7.3 0.7 %copy-done.8 = s32[1,128]{1,0:T(1,128)S(1)} copy-done((s32[1,128]{1,0:T(1,128)S(1)}, s32[1,128]{1,0:T(1,128)}, u32[]{:S(2)}) %copy-start.8) | copy-done | bytes 536
  8.0 3.6 %near_sums.1 = (f32[8,256,128]{2,1,0:T(8,128)S(1)}, f32[2048,256]{1,0:T(8,128)S(1)}, bf16[16,256,128]{2,1,0:T(8,128)(2,1)S(1)}, bf16[2048,256]{1,0:T(8,128)(2,1)...) custom-call(s32[1]{0:T(128)S(6)} %copy.9.count_ref, ...), custom_call_target="tpu_custom_call" | custom-call | bytes 24000000 | tf_op jit(solution)/shard_map/near_sums/pallas_call | solution.py:239
  11.6 0.0 collective-permute-done.1.refs_2_
  11.6 0.0 collective-permute-done.2.refs_3_
  11.7 0.0 copy-start.7
  11.7 0.0 copy-start.9
  11.7 2.5 %far_sums.1 = (f32[512,256]{1,0:T(8,128)S(1)}, f32[512,256]{1,0:T(8,128)S(1)}, bf16[128,128,128]{2,1,0:T(8,128)(2,1)S(1)}, bf16[1024,256]{1,0:T(8,128)(2,1)S(1)}) custom-call(s32[1]{0:T(128)S(6)} %copy.9.count_ref, s32[2]{0:T(128)S(1)} %pad_add_fusion.place_ref, s32[1,128]{1,0:T(1,128)S(1)} %copy-done.6, s32[1,128]{1,0:T(1,128)S(1)} %copy-done.8, ...), custom_call_target="tpu_custom_call" | custom-call | bytes 15000000 | tf_op jit(solution)/shard_map/far_sums/pallas_call | solution.py:260
  14.2 0.0 copy-start
  14.2 1.9 %copy-done = bf16[128,128,128]{2,1,0:T(8,128)(2,1)} copy-done((bf16[128,128,128]{2,1,0:T(8,128)(2,1)}, bf16[128,128,128]{2,1,0:T(8,128)(2,1)S(1)}, u32[]{:S(2)}) %copy-start) | copy-done | bytes 4194328
  16.1 0.0 copy-start.3
  16.1 0.8 %copy-done.3 = bf16[1024,256]{1,0:T(8,128)(2,1)} copy-done((bf16[1024,256]{1,0:T(8,128)(2,1)}, bf16[1024,256]{1,0:T(8,128)(2,1)S(1)}, u32[]{:S(2)}) %copy-start.3) | copy-done | bytes 524312
  16.9 5.2 %collective-permute-start.3 = (f32[512,256]{1,0:T(8,128)S(1)}, f32[512,256]{1,0:T(8,128)S(1)}, u32[]{:S(2)}, u32[]{:S(2)}) collective-permute-start(f32[512,256]{1,0:T(8,128)S(1)} %get-tuple-element.23), channel_id=1, source_target_pairs={{0,1},{1,0},{2,3},{3,2},{4,5},{5,4},{6,7},{7,6},{8,9},{9,8},{10,11... | collective-permute-start | bytes 1572872 | tf_op jit(solution)/shard_map/ppermute | solution.py:229
  22.2 1.5 %collective-permute-done.3 = f32[512,256]{1,0:T(8,128)S(1)} collective-permute-done((f32[512,256]{1,0:T(8,128)S(1)}, f32[512,256]{1,0:T(8,128)S(1)}, u32[]{:S(2)}, u32[]{:S(2)}) %collective-permute-start.3) | collective-permute-done | bytes 524320 | tf_op jit(solution)/shard_map/ppermute | solution.py:229
  23.7 0.1 add.47
  23.8 0.1 collective-permute-start.4
  23.9 3.5 %collective-permute-start.6 = (f32[128,256]{1,0:T(8,128)S(1)}, f32[128,256]{1,0:T(8,128)S(1)}, u32[]{:S(2)}, u32[]{:S(2)}) collective-permute-start(f32[128,256]{1,0:T(8,128)S(1)} %get-tuple-element.25), channel_id=1, source_target_pairs={{0,2},{1,3},{2,0},{3,1},{4,6},{5,7},{6,4},{7,5},{8,10},{9,11},{10,... | collective-permute-start | bytes 393224 | tf_op jit(solution)/shard_map/ppermute | solution.py:229
  27.4 1.1 %collective-permute-start.5 = (f32[128,256]{1,0:T(8,128)S(1)}, f32[128,256]{1,0:T(8,128)S(1)}, u32[]{:S(2)}, u32[]{:S(2)}) collective-permute-start(f32[128,256]{1,0:T(8,128)S(1)} %get-tuple-element.26), channel_id=1, source_target_pairs={{0,4},{1,5},{2,6},{3,7},{4,0},{5,1},{6,2},{7,3},{8,12},{9,13},{10,... | collective-permute-start | bytes 393224 | tf_op jit(solution)/shard_map/ppermute | solution.py:229
  28.5 2.1 %collective-permute-done.4 = f32[128,256]{1,0:T(8,128)S(1)} collective-permute-done((f32[128,256]{1,0:T(8,128)S(1)}, f32[128,256]{1,0:T(8,128)S(1)}, u32[]{:S(2)}, u32[]{:S(2)}) %collective-permute-start.4) | collective-permute-done | bytes 131104 | tf_op jit(solution)/shard_map/ppermute | solution.py:229
  30.7 2.7 %collective-permute-done.6 = f32[128,256]{1,0:T(8,128)S(1)} collective-permute-done((f32[128,256]{1,0:T(8,128)S(1)}, f32[128,256]{1,0:T(8,128)S(1)}, u32[]{:S(2)}, u32[]{:S(2)}) %collective-permute-start.6) | collective-permute-done | bytes 131104 | tf_op jit(solution)/shard_map/ppermute | solution.py:229
  33.4 1.8 %collective-permute-done.5 = f32[128,256]{1,0:T(8,128)S(1)} collective-permute-done((f32[128,256]{1,0:T(8,128)S(1)}, f32[128,256]{1,0:T(8,128)S(1)}, u32[]{:S(2)}, u32[]{:S(2)}) %collective-permute-start.5) | collective-permute-done | bytes 131104 | tf_op jit(solution)/shard_map/ppermute | solution.py:229
  35.2 3.6 %collective-permute-start.7 = (f32[32,256]{1,0:T(8,128)S(1)}, f32[32,256]{1,0:T(8,128)S(1)}, u32[]{:S(2)}, u32[]{:S(2)}) collective-permute-start(f32[32,256]{1,0:T(8,128)S(1)} %get-tuple-element.27), channel_id=1, source_target_pairs={{0,24},{1,25},{2,26},{3,27},{4,28},{5,29},{6,30},{7,31},{8,16},{9,... | collective-permute-start | bytes 98312 | tf_op jit(solution)/shard_map/ppermute | solution.py:229
  38.7 0.0 collective-permute-start.9
  38.8 0.9 %collective-permute-start.8 = (f32[32,256]{1,0:T(8,128)S(1)}, f32[32,256]{1,0:T(8,128)S(1)}, u32[]{:S(2)}, u32[]{:S(2)}) collective-permute-start(f32[32,256]{1,0:T(8,128)S(1)} %get-tuple-element.29), channel_id=1, source_target_pairs={{0,16},{1,17},{2,18},{3,19},{4,20},{5,21},{6,22},{7,23},{8,24},{9,... | collective-permute-start | bytes 98312 | tf_op jit(solution)/shard_map/ppermute | solution.py:229
  39.6 0.0 copy-done.7
  39.6 0.0 copy-done.9
  39.6 0.0 copy-start.1
  39.6 2.2 %copy-done.1 = bf16[128,128,128]{2,1,0:T(8,128)(2,1)S(1)} copy-done((bf16[128,128,128]{2,1,0:T(8,128)(2,1)S(1)}, bf16[128,128,128]{2,1,0:T(8,128)(2,1)}, u32[]{:S(2)}) %copy-start.1) | copy-done | bytes 4194328
  41.8 0.0 copy-start.4
  41.8 1.0 %copy-done.4 = bf16[1024,256]{1,0:T(8,128)(2,1)S(1)} copy-done((bf16[1024,256]{1,0:T(8,128)(2,1)S(1)}, bf16[1024,256]{1,0:T(8,128)(2,1)}, u32[]{:S(2)}) %copy-start.4) | copy-done | bytes 524312
  42.9 2.6 %user_sums.1 = f32[2048,256]{1,0:T(8,128)} custom-call(s32[1]{0:T(128)S(6)} %copy.9.count_ref, s32[2]{0:T(128)S(1)} %pad_add_fusion.place_ref, s32[1,128]{1,0:T(1,128)S(1)} %copy-done.7, s32[1,128]{1,0:T(1,128)S(1)} %copy-done.9, s32[136]{0:T(256)S(1)} %get-tuple-element.13.order_ref, f32[2048,256]{1,0:T(8,128)S(1)} %get-tuple-element.14.near_ref, ...), custom_call_target="tpu_custom_call" | custom-call | bytes 9000000 | tf_op jit(solution)/shard_map/user_sums/pallas_call | solution.py:273
  45.5 0.0 collective-permute-done.7
  45.5 0.0 collective-permute-done.9
  45.5 0.0 collective-permute-done.8
  45.5 0.6 %fusion.5 = f32[32,256]{1,0:T(8,128)} fusion(f32[32,256]{1,0:T(8,128)S(1)} %collective-permute-done.9, f32[32,256]{1,0:T(8,128)S(1)} %collective-permute-done.8, f32[32,256]{1,0:T(8,128)S(1)} %collective-permute-done.7, f32[128,256]{1,0:T(8,128)S(1)} %fusion.1, bf16[1024,256]{1,0:T(8,128)(2,1)S(1)} %copy-done.4, s32[]{:T(128)S(6)} %select_n.3), kind=kLoop, calls=%fused_computation.7 | loop fusion | flops 57344 | bytes 180228 | tf_op jit(solution)/shard_map/add | solution.py:294
  (3 shorter events, 0.1 us)
Async XLA Ops:
  0.6 3.9 %collective-permute-start = (bf16[256,256]{1,0:T(8,128)(2,1)}, bf16[256,256]{1,0:T(8,128)(2,1)S(1)}, u32[]{:S(2)}, u32[]{:S(2)}) collective-permute-start(bf16[256,256]{1,0:T(8,128)(2,1)} %refs_0_.1), channel_id=1, source_target_pairs={{0,1},{1,0},{2,3},{3,2},{4,5},{5,4},{6,7},{7,6},{8,9},{9,8},{10,11... | collective-permute-start | bytes 393224 | tf_op jit(solution)/shard_map/ppermute | solution.py:229
  1.1 10.5 %collective-permute-start.1 = (bf16[256,256]{1,0:T(8,128)(2,1)}, bf16[256,256]{1,0:T(8,128)(2,1)S(1)}, u32[]{:S(2)}, u32[]{:S(2)}) collective-permute-start(bf16[256,256]{1,0:T(8,128)(2,1)} %refs_0_.1), channel_id=1, source_target_pairs={{0,2},{1,3},{2,0},{3,1},{4,6},{5,7},{6,4},{7,5},{8,10},{9,11},{10,... | collective-permute-start | bytes 393224 | tf_op jit(solution)/shard_map/ppermute | solution.py:229
  3.7 7.9 %collective-permute-start.2 = (bf16[256,256]{1,0:T(8,128)(2,1)}, bf16[256,256]{1,0:T(8,128)(2,1)S(1)}, u32[]{:S(2)}, u32[]{:S(2)}) collective-permute-start(bf16[256,256]{1,0:T(8,128)(2,1)} %refs_0_.1), channel_id=1, source_target_pairs={{0,3},{1,2},{2,1},{3,0},{4,7},{5,6},{6,5},{7,4},{8,11},{9,10},{10,... | collective-permute-start | bytes 393224 | tf_op jit(solution)/shard_map/ppermute | solution.py:229
  4.5 1.2 %copy-start.2 = (bf16[2048,256]{1,0:T(8,128)(2,1)S(1)}, bf16[2048,256]{1,0:T(8,128)(2,1)}, u32[]{:S(2)}) copy-start(bf16[2048,256]{1,0:T(8,128)(2,1)} %user_ref.1) | copy-start | bytes 3145732
  5.8 0.9 %copy-start.5 = (bf16[256,256]{1,0:T(8,128)(2,1)S(1)}, bf16[256,256]{1,0:T(8,128)(2,1)}, u32[]{:S(2)}) copy-start(bf16[256,256]{1,0:T(8,128)(2,1)} %refs_0_.1) | copy-start | bytes 393220
  6.7 0.7 %copy-start.6 = (s32[1,128]{1,0:T(1,128)S(1)}, s32[1,128]{1,0:T(1,128)}, u32[]{:S(2)}) copy-start(s32[1,128]{1,0:T(1,128)} %user_id_ref.5) | copy-start | bytes 1540
  7.3 0.7 %copy-start.8 = (s32[1,128]{1,0:T(1,128)S(1)}, s32[1,128]{1,0:T(1,128)}, u32[]{:S(2)}) copy-start(s32[1,128]{1,0:T(1,128)} %item_id_ref.5) | copy-start | bytes 1540
  11.7 28.0 %copy-start.7 = (s32[1,128]{1,0:T(1,128)S(1)}, s32[1,128]{1,0:T(1,128)}, u32[]{:S(2)}) copy-start(s32[1,128]{1,0:T(1,128)} %user_id_ref.5) | copy-start | bytes 1540
  11.7 28.0 %copy-start.9 = (s32[1,128]{1,0:T(1,128)S(1)}, s32[1,128]{1,0:T(1,128)}, u32[]{:S(2)}) copy-start(s32[1,128]{1,0:T(1,128)} %item_id_ref.5) | copy-start | bytes 1540
  14.2 1.9 %copy-start = (bf16[128,128,128]{2,1,0:T(8,128)(2,1)}, bf16[128,128,128]{2,1,0:T(8,128)(2,1)S(1)}, u32[]{:S(2)}) copy-start(bf16[128,128,128]{2,1,0:T(8,128)(2,1)S(1)} %get-tuple-element.21.weighted_ref) | copy-start | bytes 12582916
  16.1 0.8 %copy-start.3 = (bf16[1024,256]{1,0:T(8,128)(2,1)}, bf16[1024,256]{1,0:T(8,128)(2,1)S(1)}, u32[]{:S(2)}) copy-start(bf16[1024,256]{1,0:T(8,128)(2,1)S(1)} %get-tuple-element.20.item_ref) | copy-start | bytes 1572868
  16.9 6.8 %collective-permute-start.3 = (f32[512,256]{1,0:T(8,128)S(1)}, f32[512,256]{1,0:T(8,128)S(1)}, u32[]{:S(2)}, u32[]{:S(2)}) collective-permute-start(f32[512,256]{1,0:T(8,128)S(1)} %get-tuple-element.23), channel_id=1, source_target_pairs={{0,1},{1,0},{2,3},{3,2},{4,5},{5,4},{6,7},{7,6},{8,9},{9,8},{10,11... | collective-permute-start | bytes 1572872 | tf_op jit(solution)/shard_map/ppermute | solution.py:229
  23.8 6.8 %collective-permute-start.4 = (f32[128,256]{1,0:T(8,128)S(1)}, f32[128,256]{1,0:T(8,128)S(1)}, u32[]{:S(2)}, u32[]{:S(2)}) collective-permute-start(f32[128,256]{1,0:T(8,128)S(1)} %get-tuple-element.24), channel_id=1, source_target_pairs={{0,6},{1,7},{2,4},{3,5},{4,2},{5,3},{6,0},{7,1},{8,14},{9,15},{10,... | collective-permute-start | bytes 393224 | tf_op jit(solution)/shard_map/ppermute | solution.py:229
  23.9 9.5 %collective-permute-start.6 = (f32[128,256]{1,0:T(8,128)S(1)}, f32[128,256]{1,0:T(8,128)S(1)}, u32[]{:S(2)}, u32[]{:S(2)}) collective-permute-start(f32[128,256]{1,0:T(8,128)S(1)} %get-tuple-element.25), channel_id=1, source_target_pairs={{0,2},{1,3},{2,0},{3,1},{4,6},{5,7},{6,4},{7,5},{8,10},{9,11},{10,... | collective-permute-start | bytes 393224 | tf_op jit(solution)/shard_map/ppermute | solution.py:229
  27.4 7.7 %collective-permute-start.5 = (f32[128,256]{1,0:T(8,128)S(1)}, f32[128,256]{1,0:T(8,128)S(1)}, u32[]{:S(2)}, u32[]{:S(2)}) collective-permute-start(f32[128,256]{1,0:T(8,128)S(1)} %get-tuple-element.26), channel_id=1, source_target_pairs={{0,4},{1,5},{2,6},{3,7},{4,0},{5,1},{6,2},{7,3},{8,12},{9,13},{10,... | collective-permute-start | bytes 393224 | tf_op jit(solution)/shard_map/ppermute | solution.py:229
  35.2 10.3 %collective-permute-start.7 = (f32[32,256]{1,0:T(8,128)S(1)}, f32[32,256]{1,0:T(8,128)S(1)}, u32[]{:S(2)}, u32[]{:S(2)}) collective-permute-start(f32[32,256]{1,0:T(8,128)S(1)} %get-tuple-element.27), channel_id=1, source_target_pairs={{0,24},{1,25},{2,26},{3,27},{4,28},{5,29},{6,30},{7,31},{8,16},{9,... | collective-permute-start | bytes 98312 | tf_op jit(solution)/shard_map/ppermute | solution.py:229
  38.7 6.8 %collective-permute-start.9 = (f32[32,256]{1,0:T(8,128)S(1)}, f32[32,256]{1,0:T(8,128)S(1)}, u32[]{:S(2)}, u32[]{:S(2)}) collective-permute-start(f32[32,256]{1,0:T(8,128)S(1)} %get-tuple-element.28), channel_id=1, source_target_pairs={{0,8},{1,9},{2,10},{3,11},{4,12},{5,13},{6,14},{7,15},{8,0},{9,1},... | collective-permute-start | bytes 98312 | tf_op jit(solution)/shard_map/ppermute | solution.py:229
  38.8 6.8 %collective-permute-start.8 = (f32[32,256]{1,0:T(8,128)S(1)}, f32[32,256]{1,0:T(8,128)S(1)}, u32[]{:S(2)}, u32[]{:S(2)}) collective-permute-start(f32[32,256]{1,0:T(8,128)S(1)} %get-tuple-element.29), channel_id=1, source_target_pairs={{0,16},{1,17},{2,18},{3,19},{4,20},{5,21},{6,22},{7,23},{8,24},{9,... | collective-permute-start | bytes 98312 | tf_op jit(solution)/shard_map/ppermute | solution.py:229
  39.6 2.2 %copy-start.1 = (bf16[128,128,128]{2,1,0:T(8,128)(2,1)S(1)}, bf16[128,128,128]{2,1,0:T(8,128)(2,1)}, u32[]{:S(2)}) copy-start(bf16[128,128,128]{2,1,0:T(8,128)(2,1)} %copy-done) | copy-start | bytes 12582916
  41.8 1.0 %copy-start.4 = (bf16[1024,256]{1,0:T(8,128)(2,1)S(1)}, bf16[1024,256]{1,0:T(8,128)(2,1)}, u32[]{:S(2)}) copy-start(bf16[1024,256]{1,0:T(8,128)(2,1)} %copy-done.3) | copy-start | bytes 1572868

commit v3 on v1

v3 whole, which is shorter than its diff:
```python
import functools

import jax
import jax.numpy as jnp
from jax import lax
from jax.experimental import pallas as pl
from jax.experimental.pallas import tpu as pltpu
from jax.sharding import PartitionSpec as P

grad_scale = 0.015625
decay_rate = 0.05
AXES = ("users", "items")
UNROLL = 16
VMEM = pl.BlockSpec(memory_space=pltpu.VMEM)
SMEM = pl.BlockSpec(memory_space=pltpu.SMEM)
HBM = pl.BlockSpec(memory_space=pltpu.HBM)


def phases_of(device_total):
    bit_total = device_total.bit_length() - 1
    groups = [[0]]
    for bit in range(1, bit_total, 2):
        groups.append(list(range(bit, min(bit + 2, bit_total))))
    return groups


def place_of(index, groups):
    place = 0
    for group in groups:
        for bit in reversed(group):
            place = place * 2 + ((index >> bit) & 1)
    return place


def order_kernel(entry_ref, order_ref, *, slots, near_blocks):
    stride = order_ref.shape[0] // 2
    live = entry_ref[slots]

    def sort(slot, near_total):
        entry = entry_ref[slot]
        near = (entry // 256) % 256 < near_blocks
        order_ref[jnp.where(near, near_total, stride + slot - near_total)] = entry
        return near_total + near.astype(jnp.int32)

    near_total = lax.fori_loop(0, live, sort, 0)

    def pad(index, carry):
        order_ref[near_total + index] = 0
        order_ref[stride + live - near_total + index] = 0
        return carry

    lax.fori_loop(0, UNROLL, pad, 0)
    order_ref[stride - 1] = near_total
    order_ref[2 * stride - 1] = live - near_total
    order_ref[2 * stride - 2] = entry_ref[slots + 1]


def fields(entry, block):
    return pl.multiple_of(entry // 65536 * block, block), (entry // 256) % 256, entry % 256


def add_slots(first, total_slots, order_ref, user_ref, turned_ref, item_ref, rating_ref, weight_ref, held_rating,
              held_weight, rating_sems, weight_sems, total, after):
    block = held_rating.shape[1]
    turns = (total_slots + UNROLL - 1) // UNROLL
    ahead = 3

    def start(index):
        for step in range(UNROLL):
            position = index * UNROLL + step
            slot = fields(order_ref[first + position], block)[2]
            pltpu.make_async_copy(rating_ref.at[0, slot], held_rating.at[position], rating_sems.at[index]).start()
            pltpu.make_async_copy(weight_ref.at[0, slot], held_weight.at[position], weight_sems.at[index]).start()

    def wait(index):
        part = pl.ds(index * UNROLL, UNROLL)
        pltpu.make_async_copy(rating_ref.at[0, pl.ds(0, UNROLL)], held_rating.at[part], rating_sems.at[index]).wait()
        pltpu.make_async_copy(weight_ref.at[0, pl.ds(0, UNROLL)], held_weight.at[part], weight_sems.at[index]).wait()

    def prime(index, carry):
        start(index)
        return carry

    def turn(index, carry):
        @pl.when(index + ahead < turns)
        def _():
            start(index + ahead)

        wait(index)
        base = index * UNROLL
        chosen = [fields(order_ref[first + base + step], block) for step in range(UNROLL)]
        predicted = []
        for user_row, item, _ in chosen:
            item_row = pl.multiple_of(item * block, block)
            predicted.append(lax.dot_general(
                user_ref[pl.ds(user_row, block), :], item_ref[pl.ds(item_row, block), :],
                (((1,), (1,)), ((), ())), preferred_element_type=jnp.float32))
        tiles = []
        for step in range(UNROLL):
            weighted = held_weight[base + step].astype(jnp.float32) * (
                predicted[step] - held_rating[base + step].astype(jnp.float32))
            tiles.append(jnp.where(base + step < total_slots, weighted, 0.0).astype(jnp.bfloat16))
        terms = [jnp.dot(turned_ref[entry[0] // block], tile, preferred_element_type=jnp.float32)
                 for entry, tile in zip(chosen, tiles)]
        after(index, chosen, tiles)
        for (_, item, _), term in zip(chosen, terms):
            total[item] += term
        return carry

    def prepare():
        lax.fori_loop(0, jnp.minimum(turns, ahead), prime, 0)

    def run():
        lax.fori_loop(0, turns, turn, 0)

    return prepare, run


def near_kernel(order_ref, user_ref, own_ref, pair_ref, rating_ref, weight_ref, total, user_total, turned_ref,
                held_rating, held_weight, item_ref, rating_sems, weight_sems):
    block = held_rating.shape[1]
    stride = order_ref.shape[0] // 2
    near_total = order_ref[stride - 1]

    def after(index, chosen, tiles):
        terms = []
        for (_, item, _), tile in zip(chosen, tiles):
            item_row = pl.multiple_of(item * block, block)
            terms.append(jnp.dot(tile, item_ref[pl.ds(item_row, block), :], preferred_element_type=jnp.float32))
        for (user_row, _, _), term in zip(chosen, terms):
            user_total[pl.ds(user_row, block), :] += term

    prepare, run = add_slots(0, near_total, order_ref, user_ref, turned_ref, item_ref, rating_ref, weight_ref,
                             held_rating, held_weight, rating_sems, weight_sems, total, after)
    prepare()
    item_ref[:own_ref.shape[0], :] = own_ref[...]
    item_ref[own_ref.shape[0]:, :] = pair_ref[...]
    total[...] = jnp.zeros_like(total)
    user_total[...] = jnp.zeros_like(user_total)
    for index in range(turned_ref.shape[0]):
        turned_ref[index] = user_ref[index * block:(index + 1) * block, :].T
    run()


def join(panel_refs, item_ref):
    row = 0
    for panel_ref in panel_refs:
        item_ref[row:row + panel_ref.shape[0], :] = panel_ref[...]
        row += panel_ref.shape[0]


def far_kernel(owner_total, groups, order_ref, user_ref, turned_ref, near_ref, rating_ref, weight_ref, *refs):
    panel_refs, refs = refs[:-11], refs[-11:]
    (keep_ref, send_ref, weighted_ref, held_rating, held_weight, item_ref, total, tile_ref, rating_sems,
     weight_sems, tile_sems) = refs
    block = held_rating.shape[1]
    stride = order_ref.shape[0] // 2
    far_total = order_ref[2 * stride - 1]
    turns = (far_total + UNROLL - 1) // UNROLL

    def copy_of(index):
        part = pl.ds(index * UNROLL, UNROLL)
        return pltpu.make_async_copy(tile_ref.at[part], weighted_ref.at[part], tile_sems.at[index])

    def after(index, chosen, tiles):
        for step, tile in enumerate(tiles):
            tile_ref[index * UNROLL + step] = tile
        copy_of(index).start()

    prepare, run = add_slots(stride, far_total, order_ref, user_ref, turned_ref, item_ref, rating_ref, weight_ref,
                             held_rating, held_weight, rating_sems, weight_sems, total, after)
    prepare()
    join(panel_refs, item_ref)
    total[...] = near_ref[...]
    run()
    own_place = order_ref[2 * stride - 2]
    owned = keep_ref.shape[0] * 2 // owner_total
    half = owner_total // 2
    per_block = block // owned
    for item in range(total.shape[0]):
        rows = total[item].T
        for part in range(per_block):
            place = own_place ^ place_of(item * per_block + part, groups)
            piece = rows[part * owned:(part + 1) * owned]
            row = pl.multiple_of((place % half) * owned, owned)

            @pl.when(place < half)
            def _():
                keep_ref[pl.ds(row, owned), :] = piece

            @pl.when(place >= half)
            def _():
                send_ref[pl.ds(row, owned), :] = piece

    def finish(index, carry):
        copy_of(index).wait()
        return carry

    lax.fori_loop(0, turns, finish, 0)


def user_kernel(order_ref, user_ref, near_ref, weighted_ref, *refs):
    panel_refs, (grad_ref, token_ref, tile_ref, item_ref, total_ref, tile_sems, sems) = refs[:-7], refs[-7:]
    block = tile_ref.shape[1]
    stride = order_ref.shape[0] // 2
    far_total = order_ref[2 * stride - 1]
    turns = (far_total + UNROLL - 1) // UNROLL

    def copy_of(index):
        part = pl.ds(index * UNROLL, UNROLL)
        return pltpu.make_async_copy(weighted_ref.at[part], tile_ref.at[part], tile_sems.at[index])

    def prime(index, carry):
        copy_of(index).start()
        return carry

    lax.fori_loop(0, turns, prime, 0)
    token_ref[...] = jnp.zeros_like(token_ref)
    join(panel_refs, item_ref)
    total_ref[...] = near_ref[...]

    def turn(index, carry):
        copy_of(index).wait()
        base = index * UNROLL
        chosen = [fields(order_ref[stride + base + step], block) for step in range(UNROLL)]
        terms = []
        for step, (_, item, _) in enumerate(chosen):
            item_row = pl.multiple_of(item * block, block)
            terms.append(jnp.dot(tile_ref[base + step], item_ref[pl.ds(item_row, block), :],
                                 preferred_element_type=jnp.float32))
        for (user_row, _, _), term in zip(chosen, terms):
            total_ref[pl.ds(user_row, block), :] += term
        return carry

    lax.fori_loop(0, turns, turn, 0)

    def writeback(index):
        rows = pl.ds(index * block, block)
        return pltpu.make_async_copy(total_ref.at[rows], grad_ref.at[rows], sems.at[index])

    blocks = total_ref.shape[0] // block
    for index in range(blocks):
        rows = pl.ds(index * block, block)
        total_ref[rows, :] = total_ref[rows, :] * grad_scale + decay_rate * user_ref[rows, :].astype(jnp.float32)
        writeback(index).start()
    for index in range(blocks):
        writeback(index).wait()


def body(user_factors, item_factors, block_user, block_item, counts, ratings, weights):
    rank = user_factors.shape[1]
    slots, block = ratings.shape[1], ratings.shape[2]
    user_rows = user_factors.shape[0]
    panel_rows = item_factors.shape[0]
    panel_total = lax.axis_size("items")
    device_total = lax.axis_size("users") * panel_total
    panel_index = lax.axis_index("items")
    me = lax.axis_index("users") * panel_total + panel_index
    groups = phases_of(device_total)
    item_rows = panel_rows * panel_total
    turns = slots // UNROLL

    def permute(array, mask):
        return lax.ppermute(array, AXES, [(index, index ^ mask) for index in range(device_total)])

    def options(micros):
        return dict(
            compiler_params=pltpu.CompilerParams(vmem_limit_bytes=47 << 20),
            cost_estimate=pl.CostEstimate(flops=0, bytes_accessed=int(3e6 * micros), transcendentals=0),
        )

    panels = [item_factors] + [permute(item_factors, mask) for mask in range(1, panel_total)]
    panel_blocks = panel_rows // block
    item_mask = panel_index * panel_blocks
    own_place = place_of(me ^ (item_mask * (block * device_total // item_rows)), groups)
    entries = (block_user[0] * 256 + (block_item[0] ^ item_mask)) * 256 + jnp.arange(slots, dtype=jnp.int32)
    entries = jnp.concatenate([entries, counts, own_place.astype(jnp.int32).reshape(1)])
    order = pl.pallas_call(
        functools.partial(order_kernel, slots=slots, near_blocks=2 * panel_blocks),
        out_shape=jax.ShapeDtypeStruct((2 * (slots + UNROLL + 16),), jnp.int32),
        in_specs=[SMEM],
        out_specs=SMEM,
        name="order",
        **options(4),
    )(entries)

    sums_shape = jax.ShapeDtypeStruct((item_rows // block, rank, block), jnp.float32)
    user_shape = jax.ShapeDtypeStruct((user_rows, rank), jnp.float32)
    tiles = pltpu.VMEM((slots, block, block), jnp.bfloat16)
    sems = pltpu.SemaphoreType.DMA((turns,))
    whole = pltpu.VMEM((item_rows, rank), jnp.bfloat16)
    near_sums, near_users, turned = pl.pallas_call(
        near_kernel,
        out_shape=(sums_shape, user_shape, jax.ShapeDtypeStruct((user_rows // block, rank, block), jnp.bfloat16)),
        in_specs=[SMEM] + [VMEM] * 3 + [HBM] * 2,
        out_specs=(VMEM,) * 3,
        scratch_shapes=[tiles, tiles, pltpu.VMEM((2 * panel_rows, rank), jnp.bfloat16), sems, sems],
        name="near_sums",
        **options(8),
    )(order, user_factors, panels[0], panels[1], ratings, weights)

    half_shape = jax.ShapeDtypeStruct((item_rows // 2, rank), jnp.float32)
    keep, send, weighted = pl.pallas_call(
        functools.partial(far_kernel, device_total, groups),
        out_shape=(half_shape, half_shape, jax.ShapeDtypeStruct((slots, block, block), jnp.bfloat16)),
        in_specs=[SMEM] + [VMEM] * 3 + [HBM] * 2 + [VMEM] * panel_total,
        out_specs=(VMEM, VMEM, HBM),
        scratch_shapes=[tiles, tiles, whole, pltpu.VMEM(sums_shape.shape, jnp.float32), tiles, sems, sems, sems],
        name="far_sums",
        **options(5),
    )(order, user_factors, turned, near_sums, ratings, weights, *panels)

    partial = keep + permute(send, 1)
    user_grad, token = pl.pallas_call(
        user_kernel,
        out_shape=(user_shape, jax.ShapeDtypeStruct((8, 128), jnp.float32)),
        in_specs=[SMEM] + [VMEM] * 2 + [HBM] + [VMEM] * panel_total,
        out_specs=(HBM, VMEM),
        scratch_shapes=[tiles, whole, pltpu.VMEM(user_shape.shape, user_shape.dtype), sems,
                        pltpu.SemaphoreType.DMA((user_rows // block,))],
        name="user_sums",
        **options(4),
    )(order, user_factors, near_users, weighted, *panels)
    for group in groups[1:]:
        ways = 1 << len(group)
        parts = partial.reshape(ways, -1, rank)
        partial = parts[0]
        for way in reversed(range(1, ways)):
            mask = sum(((way >> index) & 1) << bit for index, bit in enumerate(group))
            partial = partial + permute(parts[way], mask)
        if group is groups[1]:
            partial, token = lax.optimization_barrier((partial, token))
    owned_rows = partial.shape[0]
    first_row = me * owned_rows
    chosen = (first_row // panel_rows) ^ panel_index
    pieces = [lax.dynamic_slice_in_dim(panel, first_row % panel_rows, owned_rows, 0) for panel in panels]
    own_factors = pieces[0]
    for index in range(1, panel_total):
        own_factors = jnp.where(chosen == index, pieces[index], own_factors)
    item_grad = partial * grad_scale + decay_rate * own_factors.astype(jnp.float32)
    return (user_grad, item_grad)


def solution(mesh):
    in_specs = (
        P(AXES, None),
        P("items", None),
        P(AXES, None),
        P(AXES, None),
        P(AXES),
        P(AXES, None, None, None),
        P(AXES, None, None, None),
    )
    out_specs = (P(AXES, None), P(AXES, None))
    return jax.shard_map(body, mesh=mesh, in_specs=in_specs, out_specs=out_specs, check_vma=False)
```

time: 48.6 us -> 50.7 us (1.043)
  blocking collectives: 8.86 us -> 0 us
  Pallas kernels: 10.9 us -> 18.6 us
  starting transfers between devices: 9.03 us -> 13.6 us
  local copies, waits for them, and re-layouts: 8.57 us -> 5.91 us
  other arithmetic: 0.73 us -> 2.31 us
    all_gather x1 -> x0, blocking collectives: 8.86 us -> none  [body(): item_whole = lax.all_gather(item_factors, 'items', axis=0, tiled=True)]
    pallas_call x2 -> x4, Pallas kernels: 10.9 us -> 18.6 us  [the longest x1 5.58 us: body(): pl.pallas_call(functools.partial(far_kernel, device_total, groups), out_s...]
    ppermute x7 -> x10, starting transfers between devices: 9.03 us -> 13.6 us  [permute(): lax.ppermute(array, AXES, [(index, index ^ mask) for index in range(devic...]
    unnamed x14 -> x16, local copies, waits for them, and re-layouts: 6.91 us -> 5.25 us
    reshape x1 -> x0, local copies, waits for them, and re-layouts: 1.62 us -> none  [body(): turned = user_factors.reshape(-1, block, rank).swapaxes(1, 2)]
    add x1, other arithmetic: 0.63 us -> 1.45 us  [body(): partial * grad_scale + decay_rate * own_factors.astype(jnp.float32)]
    add x1 -> x2, other arithmetic: 0.03 us -> 0.71 us  [the longest x1 0.68 us: body(): (block_user[0] * 256 + (block_item[0] ^ item_mask)) * 256]
    slice x2, local copies, waits for them, and re-layouts: 0.04 us -> 0.67 us  [body(): partial = partial + permute(parts[way], mask)]
  transfers between devices with their start and end apart: 7 -> 10, of which waited for: 5 -> 3; matrix products, arithmetic and copies ran while one was open for 0% -> 2% of each run, Pallas kernels for 10% -> 26%
where the time goes in v3:
time: 50.7 us; the launch traced here: 50.1 us
  Pallas kernels  18.6 us (37%)
  starting transfers between devices  13.6 us (27%)
  waiting for transfers between devices  8.21 us (16%)
  local copies, waits for them, and re-layouts  5.91 us (12%)
  other arithmetic  2.31 us (5%)
  between operations  1.42 us (3%)
    ppermute x10, starting transfers between devices, permute(): lax.ppermute(array, AXES, [(index, index ^ mask) for index in range(devic...  13.6 us
    ppermute x10, waiting for transfers between devices, permute(): lax.ppermute(array, AXES, [(index, index ^ mask) for index in range(devic...  8.21 us
    pallas_call x1, Pallas kernels, body(): pl.pallas_call(functools.partial(far_kernel, device_total, groups), out_s...  5.58 us
    pallas_call x1, Pallas kernels, body(): pl.pallas_call(near_kernel, out_shape=(sums_shape, user_shape, jax.ShapeD...  5.26 us
    unnamed x16, local copies, waits for them, and re-layouts  5.25 us
    pallas_call x1, Pallas kernels, body(): pl.pallas_call(user_kernel, out_shape=(user_shape, jax.ShapeDtypeStruct((...  5.07 us
    pallas_call x1, Pallas kernels, body(): pl.pallas_call(functools.partial(order_kernel, slots=slots, near_blocks=2...  2.71 us
    add x1, other arithmetic, body(): partial * grad_scale + decay_rate * own_factors.astype(jnp.float32)  1.45 us
  transfers between devices with their start and end apart: 10, of which 3 were waited for; matrix products, arithmetic and copies ran while one was open for 2% of the time, Pallas kernels for 26%

profile of v3, /device:TPU:0, one launch (start us, length us, event | category | flops | bytes accessed | tf_op | source)
XLA Modules:
  0.0 50.1 jit_solution(18163241604023639738)
XLA Ops:
  0.6 0.5 %collective-permute-start = (bf16[256,256]{1,0:T(8,128)(2,1)}, bf16[256,256]{1,0:T(8,128)(2,1)S(1)}, u32[]{:S(2)}, u32[]{:S(2)}) collective-permute-start(bf16[256,256]{1,0:T(8,128)(2,1)} %refs_0_.3), channel_id=1, source_target_pairs={{0,1},{1,0},{2,3},{3,2},{4,5},{5,4},{6,7},{7,6},{8,9},{9,8},{10,11... | collective-permute-start | bytes 393224 | tf_op jit(solution)/shard_map/ppermute | solution.py:264
  1.1 2.6 %collective-permute-start.1 = (bf16[256,256]{1,0:T(8,128)(2,1)}, bf16[256,256]{1,0:T(8,128)(2,1)S(1)}, u32[]{:S(2)}, u32[]{:S(2)}) collective-permute-start(bf16[256,256]{1,0:T(8,128)(2,1)} %refs_0_.3), channel_id=1, source_target_pairs={{0,2},{1,3},{2,0},{3,1},{4,6},{5,7},{6,4},{7,5},{8,10},{9,11},{10,... | collective-permute-start | bytes 393224 | tf_op jit(solution)/shard_map/ppermute | solution.py:264
  3.7 0.1 collective-permute-start.2
  3.8 0.7 %bitcast_add_fusion = s32[128]{0:T(128)S(1)} fusion(s32[1,128]{1,0:T(1,128)} %param.10, s32[1,128]{1,0:T(1,128)} %param.9, s32[]{:T(128)S(6)} %mul.47), kind=kLoop, calls=%fused_computation.9 | loop fusion | flops 640 | bytes 1540 | tf_op jit(solution)/shard_map/add | solution.py:276
  5.1 0.1 pad_add_fusion.entry_ref
  5.2 2.7 %order.1.order_ref = s32[320]{0:T(512)S(1)} custom-call(s32[130]{0:T(256)S(1)} %pad_add_fusion.entry_ref), custom_call_target="tpu_custom_call" | custom-call | bytes 12000000 | tf_op jit(solution)/shard_map/order/pallas_call | solution.py:278
  7.9 0.0 collective-permute-done.pair_ref.refs_1_
  7.9 0.0 copy-start
  8.0 1.2 %copy-done = bf16[2048,256]{1,0:T(8,128)(2,1)S(1)} copy-done((bf16[2048,256]{1,0:T(8,128)(2,1)S(1)}, bf16[2048,256]{1,0:T(8,128)(2,1)}, u32[]{:S(2)}) %copy-start) | copy-done | bytes 1048600
  9.2 0.0 copy-start.2
  9.2 0.9 %copy-done.2 = bf16[256,256]{1,0:T(8,128)(2,1)S(1)} copy-done((bf16[256,256]{1,0:T(8,128)(2,1)S(1)}, bf16[256,256]{1,0:T(8,128)(2,1)}, u32[]{:S(2)}) %copy-start.2) | copy-done | bytes 131096
  10.1 5.3 %near_sums.1 = (f32[8,256,128]{2,1,0:T(8,128)S(1)}, f32[2048,256]{1,0:T(8,128)S(1)}, bf16[16,256,128]{2,1,0:T(8,128)(2,1)S(1)}) custom-call(s32[320]{0:T(512)S(1)} %order.1.order_ref, bf16[2048,256]{1,0:T(8,128)(2,1)S(1)} %copy-done, bf16[256,256]{1,0:T(8,128)(2,1)S(1)} %copy-done.2, bf16[256,256]{1,0:T(8,128)(2,1)S(1)} %collective-permute-done.pair_ref.refs_1_, ...), custom_call_target="tpu_custom_call" | custom-call | bytes 24000000 | tf_op jit(solution)/shard_map/near_sums/pallas_call | solution.py:292
  15.3 0.0 collective-permute-done.1.refs_2_
  15.3 0.0 collective-permute-done.2.refs_3_
  15.4 0.0 copy-start.4
  15.4 0.6 %copy-done.4 = bf16[256,256]{1,0:T(8,128)(2,1)} copy-done((bf16[256,256]{1,0:T(8,128)(2,1)}, bf16[256,256]{1,0:T(8,128)(2,1)S(1)}, u32[]{:S(2)}) %copy-start.4) | copy-done | bytes 131096
  16.0 0.0 copy-start.5
  16.0 0.9 %copy-done.5 = bf16[256,256]{1,0:T(8,128)(2,1)S(1)} copy-done((bf16[256,256]{1,0:T(8,128)(2,1)S(1)}, bf16[256,256]{1,0:T(8,128)(2,1)}, u32[]{:S(2)}) %copy-start.5) | copy-done | bytes 131096
  16.9 0.0 copy-start.1
  16.9 0.0 copy-start.3
  16.9 5.6 %far_sums.1 = (f32[512,256]{1,0:T(8,128)S(1)}, f32[512,256]{1,0:T(8,128)S(1)}, bf16[128,128,128]{2,1,0:T(8,128)(2,1)}) custom-call(s32[320]{0:T(512)S(1)} %order.1.order_ref, bf16[2048,256]{1,0:T(8,128)(2,1)S(1)} %copy-done, bf16[16,256,128]{2,1,0:T(8,128)(2,1)S(1)} %get-tuple-element.10.turned_ref, f32[8,256,128]{2,1,0:T(8,128)S(1)} %get-tuple-element.11.near_ref, ...), custom_call_target="tpu_custom_call" | custom-call | bytes 15000000 | tf_op jit(solution)/shard_map/far_sums/pallas_call | solution.py:303
  22.5 0.1 collective-permute-start.3
  22.6 1.9 %collective-permute-done.3 = f32[512,256]{1,0:T(8,128)S(1)} collective-permute-done((f32[512,256]{1,0:T(8,128)S(1)}, f32[512,256]{1,0:T(8,128)S(1)}, u32[]{:S(2)}, u32[]{:S(2)}) %collective-permute-start.3) | collective-permute-done | bytes 524320 | tf_op jit(solution)/shard_map/ppermute | solution.py:264
  24.5 0.1 add.67
  24.6 1.1 %collective-permute-start.4 = (f32[128,256]{1,0:T(8,128)S(1)}, f32[128,256]{1,0:T(8,128)S(1)}, u32[]{:S(2)}, u32[]{:S(2)}) collective-permute-start(f32[128,256]{1,0:T(8,128)S(1)} %get-tuple-element.16), channel_id=1, source_target_pairs={{0,6},{1,7},{2,4},{3,5},{4,2},{5,3},{6,0},{7,1},{8,14},{9,15},{10,... | collective-permute-start | bytes 393224 | tf_op jit(solution)/shard_map/ppermute | solution.py:264
  25.7 2.1 %collective-permute-start.5 = (f32[128,256]{1,0:T(8,128)S(1)}, f32[128,256]{1,0:T(8,128)S(1)}, u32[]{:S(2)}, u32[]{:S(2)}) collective-permute-start(f32[128,256]{1,0:T(8,128)S(1)} %get-tuple-element.18), channel_id=1, source_target_pairs={{0,4},{1,5},{2,6},{3,7},{4,0},{5,1},{6,2},{7,3},{8,12},{9,13},{10,... | collective-permute-start | bytes 393224 | tf_op jit(solution)/shard_map/ppermute | solution.py:264
  27.9 0.3 collective-permute-start.6
  28.2 3.7 %collective-permute-done.4 = f32[128,256]{1,0:T(8,128)S(1)} collective-permute-done((f32[128,256]{1,0:T(8,128)S(1)}, f32[128,256]{1,0:T(8,128)S(1)}, u32[]{:S(2)}, u32[]{:S(2)}) %collective-permute-start.4) | collective-permute-done | bytes 131104 | tf_op jit(solution)/shard_map/ppermute | solution.py:264
  31.9 2.5 %collective-permute-done.5 = f32[128,256]{1,0:T(8,128)S(1)} collective-permute-done((f32[128,256]{1,0:T(8,128)S(1)}, f32[128,256]{1,0:T(8,128)S(1)}, u32[]{:S(2)}, u32[]{:S(2)}) %collective-permute-start.5) | collective-permute-done | bytes 131104 | tf_op jit(solution)/shard_map/ppermute | solution.py:264
  34.4 0.0 collective-permute-done.6
  34.5 0.0 copy-start.7
  34.5 0.7 %copy-done.7 = f32[128,256]{1,0:T(8,128)} copy-done((f32[128,256]{1,0:T(8,128)}, f32[128,256]{1,0:T(8,128)S(1)}, u32[]{:S(2)}) %copy-start.7) | copy-done | bytes 131096
  35.2 0.6 %fusion.7 = (f32[32,256]{1,0:T(8,128)}, f32[32,256]{1,0:T(8,128)}, f32[32,256]{1,0:T(8,128)}) fusion(f32[128,256]{1,0:T(8,128)S(1)} %fusion.1), kind=kLoop, calls=%fused_computation.11 | loop fusion | bytes 196608 | tf_op jit(solution)/shard_map/slice | solution.py:330
  35.8 3.3 %collective-permute-start.7 = (f32[32,256]{1,0:T(8,128)}, f32[32,256]{1,0:T(8,128)}, u32[]{:S(2)}, u32[]{:S(2)}) collective-permute-start(f32[32,256]{1,0:T(8,128)} %get-tuple-element.19), channel_id=1, source_target_pairs={{0,24},{1,25},{2,26},{3,27},{4,28},{5,29},{6,30},{7,31},{8,16},{9,... | collective-permute-start | bytes 98312 | tf_op jit(solution)/shard_map/ppermute | solution.py:264
  39.1 3.0 %collective-permute-start.8 = (f32[32,256]{1,0:T(8,128)}, f32[32,256]{1,0:T(8,128)}, u32[]{:S(2)}, u32[]{:S(2)}) collective-permute-start(f32[32,256]{1,0:T(8,128)} %get-tuple-element.21), channel_id=1, source_target_pairs={{0,16},{1,17},{2,18},{3,19},{4,20},{5,21},{6,22},{7,23},{8,24},{9,... | collective-permute-start | bytes 98312 | tf_op jit(solution)/shard_map/ppermute | solution.py:264
  42.0 0.6 %collective-permute-start.9 = (f32[32,256]{1,0:T(8,128)}, f32[32,256]{1,0:T(8,128)}, u32[]{:S(2)}, u32[]{:S(2)}) collective-permute-start(f32[32,256]{1,0:T(8,128)} %get-tuple-element.20), channel_id=1, source_target_pairs={{0,8},{1,9},{2,10},{3,11},{4,12},{5,13},{6,14},{7,15},{8,0},{9,1},... | collective-permute-start | bytes 98312 | tf_op jit(solution)/shard_map/ppermute | solution.py:264
  42.6 0.0 copy-done.1
  42.6 0.0 copy-done.3
  42.6 0.0 copy-start.6
  42.6 0.9 %copy-done.6 = bf16[256,256]{1,0:T(8,128)(2,1)S(1)} copy-done((bf16[256,256]{1,0:T(8,128)(2,1)S(1)}, bf16[256,256]{1,0:T(8,128)(2,1)}, u32[]{:S(2)}) %copy-start.6) | copy-done | bytes 131096
  43.5 5.1 %user_sums.1 = (f32[2048,256]{1,0:T(8,128)}, f32[8,128]{1,0:T(8,128)}) custom-call(s32[320]{0:T(512)S(1)} %order.1.order_ref, bf16[2048,256]{1,0:T(8,128)(2,1)S(1)} %copy-done.1, f32[2048,256]{1,0:T(8,128)S(1)} %get-tuple-element.9.near_ref, bf16[128,128,128]{2,1,0:T(8,128)(2,1)} %get-tuple-element.12.weighted_ref, bf16[256,256]{1,0:T(8,128)(2,1)S(1)} %copy-done.3, ...), custom_call_target="tpu_custom_call" | custom-call | bytes 12000000 | tf_op jit(solution)/shard_map/user_sums/pallas_call | solution.py:314
  48.6 0.0 collective-permute-done.7
  48.6 0.0 collective-permute-done.8
  48.6 0.0 collective-permute-done.9
  48.6 1.5 %fusion.5 = f32[32,256]{1,0:T(8,128)} fusion(f32[32,256]{1,0:T(8,128)} %collective-permute-done.9, f32[32,256]{1,0:T(8,128)} %collective-permute-done.8, f32[32,256]{1,0:T(8,128)} %collective-permute-done.7, f32[128,256]{1,0:T(8,128)} %copy-done.7, bf16[256,256]{1,0:T(8,128)(2,1)S(1)} %copy-done.3, s32[]{:T(128)S(6)} %select_n.46, ...), kind=kLoop, calls=%fused_computation.7 | loop fusion | flops 81920 | bytes 229383 | tf_op jit(solution)/shard_map/add | solution.py:340
  (2 shorter events, 0.1 us)
Async XLA Ops:
  0.6 7.3 %collective-permute-start = (bf16[256,256]{1,0:T(8,128)(2,1)}, bf16[256,256]{1,0:T(8,128)(2,1)S(1)}, u32[]{:S(2)}, u32[]{:S(2)}) collective-permute-start(bf16[256,256]{1,0:T(8,128)(2,1)} %refs_0_.3), channel_id=1, source_target_pairs={{0,1},{1,0},{2,3},{3,2},{4,5},{5,4},{6,7},{7,6},{8,9},{9,8},{10,11... | collective-permute-start | bytes 393224 | tf_op jit(solution)/shard_map/ppermute | solution.py:264
  1.1 14.2 %collective-permute-start.1 = (bf16[256,256]{1,0:T(8,128)(2,1)}, bf16[256,256]{1,0:T(8,128)(2,1)S(1)}, u32[]{:S(2)}, u32[]{:S(2)}) collective-permute-start(bf16[256,256]{1,0:T(8,128)(2,1)} %refs_0_.3), channel_id=1, source_target_pairs={{0,2},{1,3},{2,0},{3,1},{4,6},{5,7},{6,4},{7,5},{8,10},{9,11},{10,... | collective-permute-start | bytes 393224 | tf_op jit(solution)/shard_map/ppermute | solution.py:264
  3.7 11.6 %collective-permute-start.2 = (bf16[256,256]{1,0:T(8,128)(2,1)}, bf16[256,256]{1,0:T(8,128)(2,1)S(1)}, u32[]{:S(2)}, u32[]{:S(2)}) collective-permute-start(bf16[256,256]{1,0:T(8,128)(2,1)} %refs_0_.3), channel_id=1, source_target_pairs={{0,3},{1,2},{2,1},{3,0},{4,7},{5,6},{6,5},{7,4},{8,11},{9,10},{10,... | collective-permute-start | bytes 393224 | tf_op jit(solution)/shard_map/ppermute | solution.py:264
  7.9 1.2 %copy-start = (bf16[2048,256]{1,0:T(8,128)(2,1)S(1)}, bf16[2048,256]{1,0:T(8,128)(2,1)}, u32[]{:S(2)}) copy-start(bf16[2048,256]{1,0:T(8,128)(2,1)} %user_ref.5) | copy-start | bytes 3145732
  9.2 0.9 %copy-start.2 = (bf16[256,256]{1,0:T(8,128)(2,1)S(1)}, bf16[256,256]{1,0:T(8,128)(2,1)}, u32[]{:S(2)}) copy-start(bf16[256,256]{1,0:T(8,128)(2,1)} %refs_0_.3) | copy-start | bytes 393220
  15.4 0.7 %copy-start.4 = (bf16[256,256]{1,0:T(8,128)(2,1)}, bf16[256,256]{1,0:T(8,128)(2,1)S(1)}, u32[]{:S(2)}) copy-start(bf16[256,256]{1,0:T(8,128)(2,1)S(1)} %collective-permute-done.2.refs_3_) | copy-start | bytes 393220
  16.0 0.9 %copy-start.5 = (bf16[256,256]{1,0:T(8,128)(2,1)S(1)}, bf16[256,256]{1,0:T(8,128)(2,1)}, u32[]{:S(2)}) copy-start(bf16[256,256]{1,0:T(8,128)(2,1)} %copy-done.4) | copy-start | bytes 393220
  16.9 25.7 %copy-start.1 = (bf16[2048,256]{1,0:T(8,128)(2,1)S(1)}, bf16[2048,256]{1,0:T(8,128)(2,1)}, u32[]{:S(2)}) copy-start(bf16[2048,256]{1,0:T(8,128)(2,1)} %user_ref.5) | copy-start | bytes 3145732
  16.9 25.7 %copy-start.3 = (bf16[256,256]{1,0:T(8,128)(2,1)S(1)}, bf16[256,256]{1,0:T(8,128)(2,1)}, u32[]{:S(2)}) copy-start(bf16[256,256]{1,0:T(8,128)(2,1)} %refs_0_.3) | copy-start | bytes 393220
  22.5 2.0 %collective-permute-start.3 = (f32[512,256]{1,0:T(8,128)S(1)}, f32[512,256]{1,0:T(8,128)S(1)}, u32[]{:S(2)}, u32[]{:S(2)}) collective-permute-start(f32[512,256]{1,0:T(8,128)S(1)} %get-tuple-element.15), channel_id=1, source_target_pairs={{0,1},{1,0},{2,3},{3,2},{4,5},{5,4},{6,7},{7,6},{8,9},{9,8},{10,11... | collective-permute-start | bytes 1572872 | tf_op jit(solution)/shard_map/ppermute | solution.py:264
  24.6 7.3 %collective-permute-start.4 = (f32[128,256]{1,0:T(8,128)S(1)}, f32[128,256]{1,0:T(8,128)S(1)}, u32[]{:S(2)}, u32[]{:S(2)}) collective-permute-start(f32[128,256]{1,0:T(8,128)S(1)} %get-tuple-element.16), channel_id=1, source_target_pairs={{0,6},{1,7},{2,4},{3,5},{4,2},{5,3},{6,0},{7,1},{8,14},{9,15},{10,... | collective-permute-start | bytes 393224 | tf_op jit(solution)/shard_map/ppermute | solution.py:264
  25.7 8.7 %collective-permute-start.5 = (f32[128,256]{1,0:T(8,128)S(1)}, f32[128,256]{1,0:T(8,128)S(1)}, u32[]{:S(2)}, u32[]{:S(2)}) collective-permute-start(f32[128,256]{1,0:T(8,128)S(1)} %get-tuple-element.18), channel_id=1, source_target_pairs={{0,4},{1,5},{2,6},{3,7},{4,0},{5,1},{6,2},{7,3},{8,12},{9,13},{10,... | collective-permute-start | bytes 393224 | tf_op jit(solution)/shard_map/ppermute | solution.py:264
  27.9 6.6 %collective-permute-start.6 = (f32[128,256]{1,0:T(8,128)S(1)}, f32[128,256]{1,0:T(8,128)S(1)}, u32[]{:S(2)}, u32[]{:S(2)}) collective-permute-start(f32[128,256]{1,0:T(8,128)S(1)} %get-tuple-element.17), channel_id=1, source_target_pairs={{0,2},{1,3},{2,0},{3,1},{4,6},{5,7},{6,4},{7,5},{8,10},{9,11},{10,... | collective-permute-start | bytes 393224 | tf_op jit(solution)/shard_map/ppermute | solution.py:264
  34.5 0.7 %copy-start.7 = (f32[128,256]{1,0:T(8,128)}, f32[128,256]{1,0:T(8,128)S(1)}, u32[]{:S(2)}) copy-start(f32[128,256]{1,0:T(8,128)S(1)} %fusion.1) | copy-start | bytes 393220
  35.8 12.8 %collective-permute-start.7 = (f32[32,256]{1,0:T(8,128)}, f32[32,256]{1,0:T(8,128)}, u32[]{:S(2)}, u32[]{:S(2)}) collective-permute-start(f32[32,256]{1,0:T(8,128)} %get-tuple-element.19), channel_id=1, source_target_pairs={{0,24},{1,25},{2,26},{3,27},{4,28},{5,29},{6,30},{7,31},{8,16},{9,... | collective-permute-start | bytes 98312 | tf_op jit(solution)/shard_map/ppermute | solution.py:264
  39.1 9.5 %collective-permute-start.8 = (f32[32,256]{1,0:T(8,128)}, f32[32,256]{1,0:T(8,128)}, u32[]{:S(2)}, u32[]{:S(2)}) collective-permute-start(f32[32,256]{1,0:T(8,128)} %get-tuple-element.21), channel_id=1, source_target_pairs={{0,16},{1,17},{2,18},{3,19},{4,20},{5,21},{6,22},{7,23},{8,24},{9,... | collective-permute-start | bytes 98312 | tf_op jit(solution)/shard_map/ppermute | solution.py:264
  42.0 6.6 %collective-permute-start.9 = (f32[32,256]{1,0:T(8,128)}, f32[32,256]{1,0:T(8,128)}, u32[]{:S(2)}, u32[]{:S(2)}) collective-permute-start(f32[32,256]{1,0:T(8,128)} %get-tuple-element.20), channel_id=1, source_target_pairs={{0,8},{1,9},{2,10},{3,11},{4,12},{5,13},{6,14},{7,15},{8,0},{9,1},... | collective-permute-start | bytes 98312 | tf_op jit(solution)/shard_map/ppermute | solution.py:264
  42.6 0.9 %copy-start.6 = (bf16[256,256]{1,0:T(8,128)(2,1)S(1)}, bf16[256,256]{1,0:T(8,128)(2,1)}, u32[]{:S(2)}) copy-start(bf16[256,256]{1,0:T(8,128)(2,1)} %copy-done.4) | copy-start | bytes 393220

commit v4 on v1

v4 whole, which is shorter than its diff:
```python
import functools

import jax
import jax.numpy as jnp
from jax import lax
from jax.experimental import pallas as pl
from jax.experimental.pallas import tpu as pltpu
from jax.sharding import PartitionSpec as P

grad_scale = 0.015625
decay_rate = 0.05
AXES = ("users", "items")
UNROLL = 16
VMEM = pl.BlockSpec(memory_space=pltpu.VMEM)
SMEM = pl.BlockSpec(memory_space=pltpu.SMEM)
HBM = pl.BlockSpec(memory_space=pltpu.HBM)


def phases_of(device_total):
    bit_total = device_total.bit_length() - 1
    groups = [[0]]
    for bit in range(1, bit_total, 2):
        groups.append(list(range(bit, min(bit + 2, bit_total))))
    return groups


def place_of(index, groups):
    place = 0
    for group in groups:
        for bit in reversed(group):
            place = place * 2 + ((index >> bit) & 1)
    return place


def stage_kernel(count_ref, user_ref, rating_ref, weight_ref, factor_ref, turned_ref, held_rating_ref, held_weight_ref,
                 factor_sem, rating_sems, weight_sems):
    slots, block = held_rating_ref.shape[0], held_rating_ref.shape[1]
    chunks = (count_ref[0] + UNROLL - 1) // UNROLL

    def copies(index):
        part = pl.ds(index * UNROLL, UNROLL)
        return (
            pltpu.make_async_copy(rating_ref.at[0, part], held_rating_ref.at[part], rating_sems.at[index]),
            pltpu.make_async_copy(weight_ref.at[0, part], held_weight_ref.at[part], weight_sems.at[index]),
        )

    factor_copy = pltpu.make_async_copy(user_ref, factor_ref, factor_sem)
    factor_copy.start()
    for index in range(slots // UNROLL):
        @pl.when(index < chunks)
        def _():
            for copy in copies(index):
                copy.start()
    factor_copy.wait()
    for index in range(turned_ref.shape[0]):
        turned_ref[index] = factor_ref[index * block:(index + 1) * block, :].T
    for index in range(slots // UNROLL):
        @pl.when(index < chunks)
        def _():
            for copy in copies(index):
                copy.wait()


def panel_copies(item_ref, spill_ref, slots, block, sem, out):
    copies = []
    for item in range(item_ref.shape[0] // block):
        for column in range(item_ref.shape[1] // block):
            here = item_ref.at[pl.ds(item * block, block), pl.ds(column * block, block)]
            there = spill_ref.at[slots + item * (item_ref.shape[1] // block) + column]
            copies.append(pltpu.make_async_copy(*((here, there) if out else (there, here)), sem))
    return copies


def item_kernel(owner_total, groups, count_ref, place_ref, user_id_ref, item_id_ref, user_ref, turned_ref, rating_ref,
                weight_ref, *refs):
    panel_refs, refs = refs[:-8], refs[-8:]
    keep_ref, send_ref, spill_ref, item_ref, total, tile_ref, tile_sems, item_sem = refs
    live = count_ref[0]
    item_mask = place_ref[1]
    slots, block = rating_ref.shape[0], rating_ref.shape[1]
    row = 0
    for panel_ref in panel_refs:
        item_ref[row:row + panel_ref.shape[0], :] = panel_ref[...]
        row += panel_ref.shape[0]
    panel_out = panel_copies(item_ref, spill_ref, slots, block, item_sem, True)
    for copy in panel_out:
        copy.start()
    total[...] = jnp.zeros_like(total)
    turns = (live + UNROLL - 1) // UNROLL

    def copy_of(index):
        part = pl.ds(index * UNROLL, UNROLL)
        return pltpu.make_async_copy(tile_ref.at[part], spill_ref.at[part], tile_sems.at[index])

    def turn(index, carry):
        base = index * UNROLL
        predicted = []
        for step in range(UNROLL):
            user_row = pl.multiple_of(user_id_ref[0, base + step] * block, block)
            item_row = pl.multiple_of((item_id_ref[0, base + step] ^ item_mask) * block, block)
            predicted.append(lax.dot_general(
                user_ref[pl.ds(user_row, block), :], item_ref[pl.ds(item_row, block), :],
                (((1,), (1,)), ((), ())), preferred_element_type=jnp.float32))
        terms = []
        for step in range(UNROLL):
            slot = base + step
            weighted = weight_ref[slot].astype(jnp.float32) * (
                predicted[step] - rating_ref[slot].astype(jnp.float32))
            weighted = jnp.where(slot < live, weighted, 0.0).astype(jnp.bfloat16)
            tile_ref[slot] = weighted
            terms.append(jnp.dot(turned_ref[user_id_ref[0, slot]], weighted, preferred_element_type=jnp.float32))
        copy_of(index).start()
        for step in range(UNROLL):
            total[item_id_ref[0, base + step]] += terms[step]
        return carry

    lax.fori_loop(0, turns, turn, 0)
    own_place = place_ref[0]
    owned = keep_ref.shape[0] * 2 // owner_total
    half = owner_total // 2
    per_block = block // owned
    for item in range(total.shape[0]):
        rows = total[item].T
        for part in range(per_block):
            place = own_place ^ place_of(item * per_block + part, groups)
            piece = rows[part * owned:(part + 1) * owned]
            row = pl.multiple_of((place % half) * owned, owned)

            @pl.when(place < half)
            def _():
                keep_ref[pl.ds(row, owned), :] = piece

            @pl.when(place >= half)
            def _():
                send_ref[pl.ds(row, owned), :] = piece

    def finish(index, carry):
        copy_of(index).wait()
        return carry

    lax.fori_loop(0, turns, finish, 0)
    for copy in panel_out:
        copy.wait()


def user_kernel(count_ref, place_ref, user_id_ref, item_id_ref, user_ref, spill_ref, grad_ref, token_ref, tile_ref,
                item_ref, total_ref, tile_sems, item_sem, sems):
    item_mask = place_ref[1]
    slots, block = tile_ref.shape[0], tile_ref.shape[1]
    turns = (count_ref[0] + UNROLL - 1) // UNROLL
    panel_in = panel_copies(item_ref, spill_ref, slots, block, item_sem, False)
    for copy in panel_in:
        copy.start()

    def copy_of(index):
        part = pl.ds(index * UNROLL, UNROLL)
        return pltpu.make_async_copy(spill_ref.at[part], tile_ref.at[part], tile_sems.at[index])

    def prime(index, carry):
        copy_of(index).start()
        return carry

    lax.fori_loop(0, turns, prime, 0)
    token_ref[...] = jnp.zeros_like(token_ref)
    total_ref[...] = jnp.zeros_like(total_ref)
    for copy in panel_in:
        copy.wait()

    def turn(index, carry):
        copy_of(index).wait()
        base = index * UNROLL
        terms = []
        for step in range(UNROLL):
            item_row = pl.multiple_of((item_id_ref[0, base + step] ^ item_mask) * block, block)
            terms.append(jnp.dot(tile_ref[base + step], item_ref[pl.ds(item_row, block), :],
                                 preferred_element_type=jnp.float32))
        for step in range(UNROLL):
            user_row = pl.multiple_of(user_id_ref[0, base + step] * block, block)
            total_ref[pl.ds(user_row, block), :] += terms[step]
        return carry

    lax.fori_loop(0, turns, turn, 0)

    def writeback(index):
        rows = pl.ds(index * block, block)
        return pltpu.make_async_copy(total_ref.at[rows], grad_ref.at[rows], sems.at[index])

    blocks = total_ref.shape[0] // block
    for index in range(blocks):
        rows = pl.ds(index * block, block)
        total_ref[rows, :] = total_ref[rows, :] * grad_scale + decay_rate * user_ref[rows, :].astype(jnp.float32)
        writeback(index).start()
    for index in range(blocks):
        writeback(index).wait()


def sum_kernel(term_total, token_ref, *refs):
    terms, parts = refs[:term_total], refs[term_total:]
    rows = parts[0].shape[0]
    for index, part in enumerate(parts):
        here = pl.ds(index * rows, rows)
        value = terms[0][here, :]
        for term in terms[1:]:
            value = value + term[here, :]
        part[...] = value.astype(part.dtype)


def sum_parts(terms, ways, token):
    rows, rank = terms[0].shape
    shape = jax.ShapeDtypeStruct((rows // ways, rank), jnp.float32)
    return pl.pallas_call(
        functools.partial(sum_kernel, len(terms)),
        out_shape=(shape,) * ways,
        in_specs=[VMEM] * (1 + len(terms)),
        out_specs=(VMEM,) * ways,
        compiler_params=pltpu.CompilerParams(vmem_limit_bytes=8 << 20),
        name="sum_parts",
    )(token, *terms)


def body(user_factors, item_factors, block_user, block_item, counts, ratings, weights):
    rank = user_factors.shape[1]
    slots, block = ratings.shape[1], ratings.shape[2]
    user_rows = user_factors.shape[0]
    panel_rows = item_factors.shape[0]
    panel_total = lax.axis_size("items")
    device_total = lax.axis_size("users") * panel_total
    panel_index = lax.axis_index("items")
    me = lax.axis_index("users") * panel_total + panel_index
    groups = phases_of(device_total)
    item_rows = panel_rows * panel_total
    turns = slots // UNROLL

    def permute(array, mask):
        return lax.ppermute(array, AXES, [(index, index ^ mask) for index in range(device_total)])

    def options(limit, micros):
        return dict(
            compiler_params=pltpu.CompilerParams(vmem_limit_bytes=limit << 20),
            cost_estimate=pl.CostEstimate(flops=0, bytes_accessed=int(3e6 * micros), transcendentals=0),
        )

    panels = [item_factors] + [permute(item_factors, mask) for mask in range(1, panel_total)]
    places = jnp.stack([place_of(me, groups), panel_index * (panel_rows // block)]).astype(jnp.int32)
    held = jax.ShapeDtypeStruct((slots, block, block), jnp.bfloat16)
    tiles = pltpu.VMEM(held.shape, held.dtype)
    sems = pltpu.SemaphoreType.DMA((turns,))
    whole = pltpu.VMEM((item_rows, rank), jnp.bfloat16)
    factors, turned, held_ratings, held_weights = pl.pallas_call(
        stage_kernel,
        out_shape=(
            jax.ShapeDtypeStruct((user_rows, rank), jnp.bfloat16),
            jax.ShapeDtypeStruct((user_rows // block, rank, block), jnp.bfloat16),
            held,
            held,
        ),
        in_specs=[SMEM] + [HBM] * 3,
        out_specs=(VMEM,) * 4,
        scratch_shapes=[pltpu.SemaphoreType.DMA, sems, sems],
        name="stage",
        **options(41, 6),
    )(counts, user_factors, ratings, weights)

    half_shape = jax.ShapeDtypeStruct((item_rows // 2, rank), jnp.float32)
    keep, send, spill = pl.pallas_call(
        functools.partial(item_kernel, device_total, groups),
        out_shape=(half_shape, half_shape, jax.ShapeDtypeStruct((6 * slots, block, block), jnp.bfloat16)),
        in_specs=[SMEM] * 4 + [VMEM] * (4 + panel_total),
        out_specs=(VMEM, VMEM, HBM),
        scratch_shapes=[whole, pltpu.VMEM((item_rows // block, rank, block), jnp.float32), tiles, sems,
                        pltpu.SemaphoreType.DMA],
        name="item_sums",
        **options(41, 8),
    )(counts, places, block_user, block_item, factors, turned, held_ratings, held_weights, *panels)

    terms = [keep, permute(send, 1)]
    user_grad, user_token = pl.pallas_call(
        user_kernel,
        out_shape=(jax.ShapeDtypeStruct((user_rows, rank), jnp.float32), jax.ShapeDtypeStruct((8, 128), jnp.float32)),
        in_specs=[SMEM] * 4 + [VMEM, HBM],
        out_specs=(HBM, VMEM),
        scratch_shapes=[tiles, whole, pltpu.VMEM((user_rows, rank), jnp.float32), sems, pltpu.SemaphoreType.DMA,
                        pltpu.SemaphoreType.DMA((user_rows // block,))],
        name="user_sums",
        **options(44, 5),
    )(counts, places, block_user, block_item, factors, spill)
    token = jnp.zeros((8, 128), jnp.float32)
    for group in groups[1:]:
        ways = 1 << len(group)
        parts = sum_parts(terms, ways, token)
        token = user_token
        terms = [parts[0]]
        for way in reversed(range(1, ways)):
            mask = sum(((way >> index) & 1) << bit for index, bit in enumerate(group))
            terms.append(permute(parts[way], mask))
    partial = functools.reduce(jnp.add, terms)
    owned_rows = partial.shape[0]
    first_row = me * owned_rows
    chosen = (first_row // panel_rows) ^ panel_index
    pieces = [lax.dynamic_slice_in_dim(panel, first_row % panel_rows, owned_rows, 0) for panel in panels]
    own_factors = pieces[0]
    for index in range(1, panel_total):
        own_factors = jnp.where(chosen == index, pieces[index], own_factors)
    item_grad = partial * grad_scale + decay_rate * own_factors.astype(jnp.float32)
    return (user_grad, item_grad)


def solution(mesh):
    in_specs = (
        P(AXES, None),
        P("items", None),
        P(AXES, None),
        P(AXES, None),
        P(AXES),
        P(AXES, None, None, None),
        P(AXES, None, None, None),
    )
    out_specs = (P(AXES, None), P(AXES, None))
    return jax.shard_map(body, mesh=mesh, in_specs=in_specs, out_specs=out_specs, check_vma=False)
```

time: 48.6 us -> 39.1 us (0.80)
  blocking collectives: 8.86 us -> 0 us
  local copies, waits for them, and re-layouts: 8.57 us -> 1.23 us
  Pallas kernels: 10.9 us -> 15.5 us
  starting transfers between devices: 9.03 us -> 12.3 us
  waiting for transfers between devices: 8.55 us -> 7.88 us
    all_gather x1 -> x0, blocking collectives: 8.86 us -> none  [body(): item_whole = lax.all_gather(item_factors, 'items', axis=0, tiled=True)]
    unnamed x14 -> x8, local copies, waits for them, and re-layouts: 6.91 us -> 1.23 us
    pallas_call x2 -> x5, Pallas kernels: 10.9 us -> 15.5 us  [the longest x1 6.3 us: body(): pl.pallas_call(functools.partial(item_kernel, device_total, groups), out_...]
    ppermute x7 -> x10, starting transfers between devices: 9.03 us -> 12.3 us  [permute(): lax.ppermute(array, AXES, [(index, index ^ mask) for index in range(devic...]
    reshape x1 -> x0, local copies, waits for them, and re-layouts: 1.62 us -> none  [body(): turned = user_factors.reshape(-1, block, rank).swapaxes(1, 2)]
    ppermute x7 -> x10, waiting for transfers between devices: 8.55 us -> 7.88 us  [permute(): lax.ppermute(array, AXES, [(index, index ^ mask) for index in range(devic...]
  transfers between devices with their start and end apart: 7 -> 10, of which waited for: 5 -> 4; matrix products, arithmetic and copies ran while one was open for 0% -> 0% of each run, Pallas kernels for 10% -> 23%
where the time goes in v4:
time: 39.1 us; the launch traced here: 38.9 us
  Pallas kernels  15.5 us (40%)
  starting transfers between devices  12.3 us (31%)
  waiting for transfers between devices  7.88 us (20%)
  between operations  1.37 us (4%)
  local copies, waits for them, and re-layouts  1.23 us (3%)
  other arithmetic  0.72 us (2%)
    ppermute x10, starting transfers between devices, permute(): lax.ppermute(array, AXES, [(index, index ^ mask) for index in range(devic...  12.3 us
    ppermute x10, waiting for transfers between devices, permute(): lax.ppermute(array, AXES, [(index, index ^ mask) for index in range(devic...  7.88 us
    pallas_call x1, Pallas kernels, body(): pl.pallas_call(functools.partial(item_kernel, device_total, groups), out_...  6.3 us
    pallas_call x1, Pallas kernels, body(): pl.pallas_call(user_kernel, out_shape=(jax.ShapeDtypeStruct((user_rows, r...  6.04 us
    pallas_call x1, Pallas kernels, body(): pl.pallas_call(stage_kernel, out_shape=(jax.ShapeDtypeStruct((user_rows,...  3.01 us
    unnamed x8, local copies, waits for them, and re-layouts  1.23 us
  transfers between devices with their start and end apart: 10, of which 4 were waited for; matrix products, arithmetic and copies ran while one was open for 0% of the time, Pallas kernels for 23%

profile of v4, /device:TPU:0, one launch (start us, length us, event | category | flops | bytes accessed | tf_op | source)
XLA Modules:
  0.0 38.9 jit_solution(6275425181275218140)
XLA Ops:
  0.6 0.5 %collective-permute-start = (bf16[256,256]{1,0:T(8,128)(2,1)}, bf16[256,256]{1,0:T(8,128)(2,1)S(1)}, u32[]{:S(2)}, u32[]{:S(2)}) collective-permute-start(bf16[256,256]{1,0:T(8,128)(2,1)} %refs_0_.1), channel_id=1, source_target_pairs={{0,1},{1,0},{2,3},{3,2},{4,5},{5,4},{6,7},{7,6},{8,9},{9,8},{10,11... | collective-permute-start | bytes 393224 | tf_op jit(solution)/shard_map/ppermute | solution.py:235
  1.1 2.6 %collective-permute-start.1 = (bf16[256,256]{1,0:T(8,128)(2,1)}, bf16[256,256]{1,0:T(8,128)(2,1)S(1)}, u32[]{:S(2)}, u32[]{:S(2)}) collective-permute-start(bf16[256,256]{1,0:T(8,128)(2,1)} %refs_0_.1), channel_id=1, source_target_pairs={{0,2},{1,3},{2,0},{3,1},{4,6},{5,7},{6,4},{7,5},{8,10},{9,11},{10,... | collective-permute-start | bytes 393224 | tf_op jit(solution)/shard_map/ppermute | solution.py:235
  3.7 0.1 collective-permute-start.2
  4.5 0.0 copy-start
  4.5 1.2 %copy-done = bf16[2048,256]{1,0:T(8,128)(2,1)S(1)} copy-done((bf16[2048,256]{1,0:T(8,128)(2,1)S(1)}, bf16[2048,256]{1,0:T(8,128)(2,1)}, u32[]{:S(2)}) %copy-start) | copy-done | bytes 1048600
  5.7 0.0 copy-start.1
  5.7 0.0 copy-start.2
  5.7 0.0 copy-start.3
  5.7 3.0 %stage.1 = (bf16[2048,256]{1,0:T(8,128)(2,1)S(1)}, bf16[16,256,128]{2,1,0:T(8,128)(2,1)S(1)}, bf16[128,128,128]{2,1,0:T(8,128)(2,1)S(1)}, bf16[128,128,128]{2,1,0:T(8,128)(2,1)S(1)}) custom-call(s32[1]{0:T(128)S(6)} %copy.9.count_ref, bf16[2048,256]{1,0:T(8,128)(2,1)S(1)} %copy-done, bf16[1,128,128,128]{3,2,1,0:T(8,128)(2,1)} %rating_ref.1, ...), custom_call_target="tpu_custom_call" | custom-call | bytes 18000000 | tf_op jit(solution)/shard_map/stage/pallas_call | solution.py:249
  8.7 0.1 pad_add_fusion.place_ref
  8.8 0.0 collective-permute-done.refs_1_
  8.8 0.0 collective-permute-done.1.refs_2_
  8.8 1.8 %collective-permute-done.2.refs_3_ = bf16[256,256]{1,0:T(8,128)(2,1)S(1)} collective-permute-done((bf16[256,256]{1,0:T(8,128)(2,1)}, bf16[256,256]{1,0:T(8,128)(2,1)S(1)}, u32[]{:S(2)}, u32[]{:S(2)}) %collective-permute-start.2) | collective-permute-done | bytes 131104 | tf_op jit(solution)/shard_map/ppermute | solution.py:235
  10.6 0.0 copy-done.1
  10.6 0.0 copy-done.2
  10.6 0.0 copy-done.3
  10.6 6.3 %item_sums.1 = (f32[512,256]{1,0:T(8,128)S(1)}, f32[512,256]{1,0:T(8,128)S(1)}, bf16[768,128,128]{2,1,0:T(8,128)(2,1)}) custom-call(s32[1]{0:T(128)S(6)} %copy.9.count_ref, s32[2]{0:T(128)S(1)} %pad_add_fusion.place_ref, s32[1,128]{1,0:T(1,128)S(1)} %copy-done.2, s32[1,128]{1,0:T(1,128)S(1)} %copy-done.3, bf16[2048,256]{1,0:T(8,128)(2,1)S(1)} %get-tuple-element.19.user_ref, ...), custom_call_target="tpu_custom_call" | custom-call | bytes 24000000 | tf_op jit(solution)/shard_map/item_sums/pallas_call | solution.py:265
  16.9 0.1 collective-permute-start.3
  17.0 1.9 %collective-permute-done.3.refs_1_ = f32[512,256]{1,0:T(8,128)S(1)} collective-permute-done((f32[512,256]{1,0:T(8,128)S(1)}, f32[512,256]{1,0:T(8,128)S(1)}, u32[]{:S(2)}, u32[]{:S(2)}) %collective-permute-start.3) | collective-permute-done | bytes 524320 | tf_op jit(solution)/shard_map/ppermute | solution.py:235
  18.9 0.1 sum_parts.2
  19.0 3.2 %collective-permute-start.4 = (f32[128,256]{1,0:T(8,128)S(1)}, f32[128,256]{1,0:T(8,128)S(1)}, u32[]{:S(2)}, u32[]{:S(2)}) collective-permute-start(f32[128,256]{1,0:T(8,128)S(1)} %get-tuple-element.29), channel_id=1, source_target_pairs={{0,6},{1,7},{2,4},{3,5},{4,2},{5,3},{6,0},{7,1},{8,14},{9,15},{10,... | collective-permute-start | bytes 393224 | tf_op jit(solution)/shard_map/ppermute | solution.py:235
  22.2 0.0 collective-permute-start.5
  22.2 1.3 %collective-permute-start.6 = (f32[128,256]{1,0:T(8,128)S(1)}, f32[128,256]{1,0:T(8,128)S(1)}, u32[]{:S(2)}, u32[]{:S(2)}) collective-permute-start(f32[128,256]{1,0:T(8,128)S(1)} %get-tuple-element.31), channel_id=1, source_target_pairs={{0,2},{1,3},{2,0},{3,1},{4,6},{5,7},{6,4},{7,5},{8,10},{9,11},{10,... | collective-permute-start | bytes 393224 | tf_op jit(solution)/shard_map/ppermute | solution.py:235
  23.5 6.0 %user_sums.1 = (f32[2048,256]{1,0:T(8,128)}, f32[8,128]{1,0:T(8,128)S(1)}) custom-call(s32[1]{0:T(128)S(6)} %copy.9.count_ref, s32[2]{0:T(128)S(1)} %pad_add_fusion.place_ref, s32[1,128]{1,0:T(1,128)S(1)} %copy-done.2, s32[1,128]{1,0:T(1,128)S(1)} %copy-done.3, bf16[2048,256]{1,0:T(8,128)(2,1)S(1)} %get-tuple-element.19.user_ref, ...), custom_call_target="tpu_custom_call" | custom-call | bytes 15000000 | tf_op jit(solution)/shard_map/user_sums/pallas_call | solution.py:277
  29.6 0.0 collective-permute-done.4.refs_1_
  29.6 0.0 collective-permute-done.5.refs_2_
  29.6 0.0 collective-permute-done.6.refs_3_
  29.6 3.8 %collective-permute-start.7 = (f32[32,256]{1,0:T(8,128)S(1)}, f32[32,256]{1,0:T(8,128)S(1)}, u32[]{:S(2)}, u32[]{:S(2)}) collective-permute-start(f32[32,256]{1,0:T(8,128)S(1)} %get-tuple-element.33), channel_id=1, source_target_pairs={{0,24},{1,25},{2,26},{3,27},{4,28},{5,29},{6,30},{7,31},{8,16},{9,... | collective-permute-start | bytes 98312 | tf_op jit(solution)/shard_map/ppermute | solution.py:235
  33.5 0.0 collective-permute-start.8
  33.5 0.6 %collective-permute-start.9 = (f32[32,256]{1,0:T(8,128)S(1)}, f32[32,256]{1,0:T(8,128)S(1)}, u32[]{:S(2)}, u32[]{:S(2)}) collective-permute-start(f32[32,256]{1,0:T(8,128)S(1)} %get-tuple-element.35), channel_id=1, source_target_pairs={{0,8},{1,9},{2,10},{3,11},{4,12},{5,13},{6,14},{7,15},{8,0},{9,1},... | collective-permute-start | bytes 98312 | tf_op jit(solution)/shard_map/ppermute | solution.py:235
  34.1 1.5 %collective-permute-done.7 = f32[32,256]{1,0:T(8,128)S(1)} collective-permute-done((f32[32,256]{1,0:T(8,128)S(1)}, f32[32,256]{1,0:T(8,128)S(1)}, u32[]{:S(2)}, u32[]{:S(2)}) %collective-permute-start.7) | collective-permute-done | bytes 32800 | tf_op jit(solution)/shard_map/ppermute | solution.py:235
  35.6 2.7 %collective-permute-done.8 = f32[32,256]{1,0:T(8,128)S(1)} collective-permute-done((f32[32,256]{1,0:T(8,128)S(1)}, f32[32,256]{1,0:T(8,128)S(1)}, u32[]{:S(2)}, u32[]{:S(2)}) %collective-permute-start.8) | collective-permute-done | bytes 32800 | tf_op jit(solution)/shard_map/ppermute | solution.py:235
  38.3 0.0 collective-permute-done.9
  38.3 0.6 %multiply_add_fusion = f32[32,256]{1,0:T(8,128)} fusion(f32[32,256]{1,0:T(8,128)S(1)} %collective-permute-done.9, f32[32,256]{1,0:T(8,128)S(1)} %collective-permute-done.8, f32[32,256]{1,0:T(8,128)S(1)} %get-tuple-element.32, f32[32,256]{1,0:T(8,128)S(1)} %collective-permute-done.7, bf16[256,256]{1,0:T(8,128)(2,1)S(1)} %copy-done.1, s32[]{:T(128)S(6)} %select_n.46, ...), kind=kLoop, calls=%fused_computation | loop fusion | flops 81920 | bytes 229383 | tf_op jit(solution)/shard_map/add | solution.py:304
  (2 shorter events, 0.0 us)
Async XLA Ops:
  0.6 8.2 %collective-permute-start = (bf16[256,256]{1,0:T(8,128)(2,1)}, bf16[256,256]{1,0:T(8,128)(2,1)S(1)}, u32[]{:S(2)}, u32[]{:S(2)}) collective-permute-start(bf16[256,256]{1,0:T(8,128)(2,1)} %refs_0_.1), channel_id=1, source_target_pairs={{0,1},{1,0},{2,3},{3,2},{4,5},{5,4},{6,7},{7,6},{8,9},{9,8},{10,11... | collective-permute-start | bytes 393224 | tf_op jit(solution)/shard_map/ppermute | solution.py:235
  1.1 7.6 %collective-permute-start.1 = (bf16[256,256]{1,0:T(8,128)(2,1)}, bf16[256,256]{1,0:T(8,128)(2,1)S(1)}, u32[]{:S(2)}, u32[]{:S(2)}) collective-permute-start(bf16[256,256]{1,0:T(8,128)(2,1)} %refs_0_.1), channel_id=1, source_target_pairs={{0,2},{1,3},{2,0},{3,1},{4,6},{5,7},{6,4},{7,5},{8,10},{9,11},{10,... | collective-permute-start | bytes 393224 | tf_op jit(solution)/shard_map/ppermute | solution.py:235
  3.7 6.8 %collective-permute-start.2 = (bf16[256,256]{1,0:T(8,128)(2,1)}, bf16[256,256]{1,0:T(8,128)(2,1)S(1)}, u32[]{:S(2)}, u32[]{:S(2)}) collective-permute-start(bf16[256,256]{1,0:T(8,128)(2,1)} %refs_0_.1), channel_id=1, source_target_pairs={{0,3},{1,2},{2,1},{3,0},{4,7},{5,6},{6,5},{7,4},{8,11},{9,10},{10,... | collective-permute-start | bytes 393224 | tf_op jit(solution)/shard_map/ppermute | solution.py:235
  4.5 1.2 %copy-start = (bf16[2048,256]{1,0:T(8,128)(2,1)S(1)}, bf16[2048,256]{1,0:T(8,128)(2,1)}, u32[]{:S(2)}) copy-start(bf16[2048,256]{1,0:T(8,128)(2,1)} %user_ref.1) | copy-start | bytes 3145732
  5.7 4.9 %copy-start.1 = (bf16[256,256]{1,0:T(8,128)(2,1)S(1)}, bf16[256,256]{1,0:T(8,128)(2,1)}, u32[]{:S(2)}) copy-start(bf16[256,256]{1,0:T(8,128)(2,1)} %refs_0_.1) | copy-start | bytes 393220
  5.7 4.9 %copy-start.2 = (s32[1,128]{1,0:T(1,128)S(1)}, s32[1,128]{1,0:T(1,128)}, u32[]{:S(2)}) copy-start(s32[1,128]{1,0:T(1,128)} %user_id_ref.3) | copy-start | bytes 1540
  5.7 4.9 %copy-start.3 = (s32[1,128]{1,0:T(1,128)S(1)}, s32[1,128]{1,0:T(1,128)}, u32[]{:S(2)}) copy-start(s32[1,128]{1,0:T(1,128)} %item_id_ref.3) | copy-start | bytes 1540
  16.9 2.0 %collective-permute-start.3 = (f32[512,256]{1,0:T(8,128)S(1)}, f32[512,256]{1,0:T(8,128)S(1)}, u32[]{:S(2)}, u32[]{:S(2)}) collective-permute-start(f32[512,256]{1,0:T(8,128)S(1)} %get-tuple-element.27), channel_id=1, source_target_pairs={{0,1},{1,0},{2,3},{3,2},{4,5},{5,4},{6,7},{7,6},{8,9},{9,8},{10,11... | collective-permute-start | bytes 1572872 | tf_op jit(solution)/shard_map/ppermute | solution.py:235
  19.0 10.6 %collective-permute-start.4 = (f32[128,256]{1,0:T(8,128)S(1)}, f32[128,256]{1,0:T(8,128)S(1)}, u32[]{:S(2)}, u32[]{:S(2)}) collective-permute-start(f32[128,256]{1,0:T(8,128)S(1)} %get-tuple-element.29), channel_id=1, source_target_pairs={{0,6},{1,7},{2,4},{3,5},{4,2},{5,3},{6,0},{7,1},{8,14},{9,15},{10,... | collective-permute-start | bytes 393224 | tf_op jit(solution)/shard_map/ppermute | solution.py:235
  22.2 7.4 %collective-permute-start.5 = (f32[128,256]{1,0:T(8,128)S(1)}, f32[128,256]{1,0:T(8,128)S(1)}, u32[]{:S(2)}, u32[]{:S(2)}) collective-permute-start(f32[128,256]{1,0:T(8,128)S(1)} %get-tuple-element.30), channel_id=1, source_target_pairs={{0,4},{1,5},{2,6},{3,7},{4,0},{5,1},{6,2},{7,3},{8,12},{9,13},{10,... | collective-permute-start | bytes 393224 | tf_op jit(solution)/shard_map/ppermute | solution.py:235
  22.2 7.4 %collective-permute-start.6 = (f32[128,256]{1,0:T(8,128)S(1)}, f32[128,256]{1,0:T(8,128)S(1)}, u32[]{:S(2)}, u32[]{:S(2)}) collective-permute-start(f32[128,256]{1,0:T(8,128)S(1)} %get-tuple-element.31), channel_id=1, source_target_pairs={{0,2},{1,3},{2,0},{3,1},{4,6},{5,7},{6,4},{7,5},{8,10},{9,11},{10,... | collective-permute-start | bytes 393224 | tf_op jit(solution)/shard_map/ppermute | solution.py:235
  29.6 6.0 %collective-permute-start.7 = (f32[32,256]{1,0:T(8,128)S(1)}, f32[32,256]{1,0:T(8,128)S(1)}, u32[]{:S(2)}, u32[]{:S(2)}) collective-permute-start(f32[32,256]{1,0:T(8,128)S(1)} %get-tuple-element.33), channel_id=1, source_target_pairs={{0,24},{1,25},{2,26},{3,27},{4,28},{5,29},{6,30},{7,31},{8,16},{9,... | collective-permute-start | bytes 98312 | tf_op jit(solution)/shard_map/ppermute | solution.py:235
  33.5 4.8 %collective-permute-start.8 = (f32[32,256]{1,0:T(8,128)S(1)}, f32[32,256]{1,0:T(8,128)S(1)}, u32[]{:S(2)}, u32[]{:S(2)}) collective-permute-start(f32[32,256]{1,0:T(8,128)S(1)} %get-tuple-element.34), channel_id=1, source_target_pairs={{0,16},{1,17},{2,18},{3,19},{4,20},{5,21},{6,22},{7,23},{8,24},{9,... | collective-permute-start | bytes 98312 | tf_op jit(solution)/shard_map/ppermute | solution.py:235
  33.5 4.8 %collective-permute-start.9 = (f32[32,256]{1,0:T(8,128)S(1)}, f32[32,256]{1,0:T(8,128)S(1)}, u32[]{:S(2)}, u32[]{:S(2)}) collective-permute-start(f32[32,256]{1,0:T(8,128)S(1)} %get-tuple-element.35), channel_id=1, source_target_pairs={{0,8},{1,9},{2,10},{3,11},{4,12},{5,13},{6,14},{7,15},{8,0},{9,1},... | collective-permute-start | bytes 98312 | tf_op jit(solution)/shard_map/ppermute | solution.py:235

commit v5 on v4

--- a/solution.py
+++ b/solution.py
@@ -11,6 +11,7 @@
 decay_rate = 0.05
 AXES = ("users", "items")
 UNROLL = 16
+WIDE = 32
 VMEM = pl.BlockSpec(memory_space=pltpu.VMEM)
 SMEM = pl.BlockSpec(memory_space=pltpu.SMEM)
 HBM = pl.BlockSpec(memory_space=pltpu.HBM)
@@ -61,20 +62,10 @@
                 copy.wait()
 
 
-def panel_copies(item_ref, spill_ref, slots, block, sem, out):
-    copies = []
-    for item in range(item_ref.shape[0] // block):
-        for column in range(item_ref.shape[1] // block):
-            here = item_ref.at[pl.ds(item * block, block), pl.ds(column * block, block)]
-            there = spill_ref.at[slots + item * (item_ref.shape[1] // block) + column]
-            copies.append(pltpu.make_async_copy(*((here, there) if out else (there, here)), sem))
-    return copies
-
-
 def item_kernel(owner_total, groups, count_ref, place_ref, user_id_ref, item_id_ref, user_ref, turned_ref, rating_ref,
                 weight_ref, *refs):
-    panel_refs, refs = refs[:-8], refs[-8:]
-    keep_ref, send_ref, spill_ref, item_ref, total, tile_ref, tile_sems, item_sem = refs
+    panel_refs, refs = refs[:-5], refs[-5:]
+    keep_ref, send_ref, tile_ref, item_ref, total = refs
     live = count_ref[0]
     item_mask = place_ref[1]
     slots, block = rating_ref.shape[0], rating_ref.shape[1]
@@ -82,35 +73,27 @@
     for panel_ref in panel_refs:
         item_ref[row:row + panel_ref.shape[0], :] = panel_ref[...]
         row += panel_ref.shape[0]
-    panel_out = panel_copies(item_ref, spill_ref, slots, block, item_sem, True)
-    for copy in panel_out:
-        copy.start()
     total[...] = jnp.zeros_like(total)
-    turns = (live + UNROLL - 1) // UNROLL
-
-    def copy_of(index):
-        part = pl.ds(index * UNROLL, UNROLL)
-        return pltpu.make_async_copy(tile_ref.at[part], spill_ref.at[part], tile_sems.at[index])
+    turns = (live + WIDE - 1) // WIDE
 
     def turn(index, carry):
-        base = index * UNROLL
+        base = index * WIDE
         predicted = []
-        for step in range(UNROLL):
+        for step in range(WIDE):
             user_row = pl.multiple_of(user_id_ref[0, base + step] * block, block)
             item_row = pl.multiple_of((item_id_ref[0, base + step] ^ item_mask) * block, block)
             predicted.append(lax.dot_general(
                 user_ref[pl.ds(user_row, block), :], item_ref[pl.ds(item_row, block), :],
                 (((1,), (1,)), ((), ())), preferred_element_type=jnp.float32))
         terms = []
-        for step in range(UNROLL):
+        for step in range(WIDE):
             slot = base + step
             weighted = weight_ref[slot].astype(jnp.float32) * (
                 predicted[step] - rating_ref[slot].astype(jnp.float32))
             weighted = jnp.where(slot < live, weighted, 0.0).astype(jnp.bfloat16)
             tile_ref[slot] = weighted
             terms.append(jnp.dot(turned_ref[user_id_ref[0, slot]], weighted, preferred_element_type=jnp.float32))
-        copy_of(index).start()
-        for step in range(UNROLL):
+        for step in range(WIDE):
             total[item_id_ref[0, base + step]] += terms[step]
         return carry
 
@@ -134,47 +117,23 @@
             def _():
                 send_ref[pl.ds(row, owned), :] = piece
 
-    def finish(index, carry):
-        copy_of(index).wait()
-        return carry
-
-    lax.fori_loop(0, turns, finish, 0)
-    for copy in panel_out:
-        copy.wait()
-
-
-def user_kernel(count_ref, place_ref, user_id_ref, item_id_ref, user_ref, spill_ref, grad_ref, token_ref, tile_ref,
-                item_ref, total_ref, tile_sems, item_sem, sems):
+
+def user_kernel(count_ref, place_ref, user_id_ref, item_id_ref, user_ref, item_ref, tile_ref, grad_ref, token_ref,
+                total_ref, sems):
     item_mask = place_ref[1]
-    slots, block = tile_ref.shape[0], tile_ref.shape[1]
-    turns = (count_ref[0] + UNROLL - 1) // UNROLL
-    panel_in = panel_copies(item_ref, spill_ref, slots, block, item_sem, False)
-    for copy in panel_in:
-        copy.start()
-
-    def copy_of(index):
-        part = pl.ds(index * UNROLL, UNROLL)
-        return pltpu.make_async_copy(spill_ref.at[part], tile_ref.at[part], tile_sems.at[index])
-
-    def prime(index, carry):
-        copy_of(index).start()
-        return carry
-
-    lax.fori_loop(0, turns, prime, 0)
+    block = tile_ref.shape[1]
+    turns = (count_ref[0] + WIDE - 1) // WIDE
     token_ref[...] = jnp.zeros_like(token_ref)
     total_ref[...] = jnp.zeros_like(total_ref)
-    for copy in panel_in:
-        copy.wait()
 
     def turn(index, carry):
-        copy_of(index).wait()
-        base = index * UNROLL
+        base = index * WIDE
         terms = []
-        for step in range(UNROLL):
+        for step in range(WIDE):
             item_row = pl.multiple_of((item_id_ref[0, base + step] ^ item_mask) * block, block)
             terms.append(jnp.dot(tile_ref[base + step], item_ref[pl.ds(item_row, block), :],
                                  preferred_element_type=jnp.float32))
-        for step in range(UNROLL):
+        for step in range(WIDE):
             user_row = pl.multiple_of(user_id_ref[0, base + step] * block, block)
             total_ref[pl.ds(user_row, block), :] += terms[step]
         return carry
@@ -243,9 +202,7 @@
     panels = [item_factors] + [permute(item_factors, mask) for mask in range(1, panel_total)]
     places = jnp.stack([place_of(me, groups), panel_index * (panel_rows // block)]).astype(jnp.int32)
     held = jax.ShapeDtypeStruct((slots, block, block), jnp.bfloat16)
-    tiles = pltpu.VMEM(held.shape, held.dtype)
     sems = pltpu.SemaphoreType.DMA((turns,))
-    whole = pltpu.VMEM((item_rows, rank), jnp.bfloat16)
     factors, turned, held_ratings, held_weights = pl.pallas_call(
         stage_kernel,
         out_shape=(
@@ -262,28 +219,26 @@
     )(counts, user_factors, ratings, weights)
 
     half_shape = jax.ShapeDtypeStruct((item_rows // 2, rank), jnp.float32)
-    keep, send, spill = pl.pallas_call(
+    keep, send, weighted, item_whole = pl.pallas_call(
         functools.partial(item_kernel, device_total, groups),
-        out_shape=(half_shape, half_shape, jax.ShapeDtypeStruct((6 * slots, block, block), jnp.bfloat16)),
+        out_shape=(half_shape, half_shape, held, jax.ShapeDtypeStruct((item_rows, rank), jnp.bfloat16)),
         in_specs=[SMEM] * 4 + [VMEM] * (4 + panel_total),
-        out_specs=(VMEM, VMEM, HBM),
-        scratch_shapes=[whole, pltpu.VMEM((item_rows // block, rank, block), jnp.float32), tiles, sems,
-                        pltpu.SemaphoreType.DMA],
+        out_specs=(VMEM,) * 4,
+        scratch_shapes=[pltpu.VMEM((item_rows // block, rank, block), jnp.float32)],
         name="item_sums",
-        **options(41, 8),
+        **options(12, 8),
     )(counts, places, block_user, block_item, factors, turned, held_ratings, held_weights, *panels)
 
     terms = [keep, permute(send, 1)]
     user_grad, user_token = pl.pallas_call(
         user_kernel,
         out_shape=(jax.ShapeDtypeStruct((user_rows, rank), jnp.float32), jax.ShapeDtypeStruct((8, 128), jnp.float32)),
-        in_specs=[SMEM] * 4 + [VMEM, HBM],
+        in_specs=[SMEM] * 4 + [VMEM] * 3,
         out_specs=(HBM, VMEM),
-        scratch_shapes=[tiles, whole, pltpu.VMEM((user_rows, rank), jnp.float32), sems, pltpu.SemaphoreType.DMA,
-                        pltpu.SemaphoreType.DMA((user_rows // block,))],
+        scratch_shapes=[pltpu.VMEM((user_rows, rank), jnp.float32), pltpu.SemaphoreType.DMA((user_rows // block,))],
         name="user_sums",
-        **options(44, 5),
-    )(counts, places, block_user, block_item, factors, spill)
+        **options(8, 5),
+    )(counts, places, block_user, block_item, factors, item_whole, weighted)
     token = jnp.zeros((8, 128), jnp.float32)
     for group in groups[1:]:
         ways = 1 << len(group)

time: 39.1 us -> 37.3 us (0.954)
  Pallas kernels: 15.5 us -> 7.41 us
  waiting for transfers between devices: 7.88 us -> 11.2 us
  starting transfers between devices: 12.3 us -> 14.9 us
    ppermute x10, waiting for transfers between devices: 7.88 us -> 11.2 us  [permute(): lax.ppermute(array, AXES, [(index, index ^ mask) for index in range(devic...]
    pallas_call x1, Pallas kernels: 6.3 us -> 3.01 us  [body(): pl.pallas_call(functools.partial(item_kernel, device_total, groups), out_...]
    pallas_call x1, Pallas kernels: 6.04 us -> 2.87 us  [body(): pl.pallas_call(user_kernel, out_shape=(jax.ShapeDtypeStruct((user_rows, r...]
    ppermute x10, starting transfers between devices: 12.3 us -> 14.9 us  [permute(): lax.ppermute(array, AXES, [(index, index ^ mask) for index in range(devic...]
    pallas_call x1, Pallas kernels: 3.01 us -> 1.44 us  [body(): pl.pallas_call(stage_kernel, out_shape=(jax.ShapeDtypeStruct((user_rows,...]
  transfers between devices with their start and end apart: 10 -> 10, of which waited for: 4 -> 7; matrix products, arithmetic and copies ran while one was open for 0% -> 0% of each run, Pallas kernels for 23% -> 12%
where the time goes in v5:
time: 37.3 us; the launch traced here: 36.8 us
  starting transfers between devices  14.9 us (40%)
  waiting for transfers between devices  11.2 us (30%)
  Pallas kernels  7.41 us (20%)
  between operations  1.35 us (4%)
  local copies, waits for them, and re-layouts  1.23 us (3%)
  other arithmetic  0.71 us (2%)
    ppermute x10, starting transfers between devices, permute(): lax.ppermute(array, AXES, [(index, index ^ mask) for index in range(devic...  14.9 us
    ppermute x10, waiting for transfers between devices, permute(): lax.ppermute(array, AXES, [(index, index ^ mask) for index in range(devic...  11.2 us
    pallas_call x1, Pallas kernels, body(): pl.pallas_call(functools.partial(item_kernel, device_total, groups), out_...  3.01 us
    pallas_call x1, Pallas kernels, body(): pl.pallas_call(user_kernel, out_shape=(jax.ShapeDtypeStruct((user_rows, r...  2.87 us
    pallas_call x1, Pallas kernels, body(): pl.pallas_call(stage_kernel, out_shape=(jax.ShapeDtypeStruct((user_rows,...  1.44 us
    unnamed x8, local copies, waits for them, and re-layouts  1.23 us
  transfers between devices with their start and end apart: 10, of which 7 were waited for; matrix products, arithmetic and copies ran while one was open for 0% of the time, Pallas kernels for 12%

profile of v5, /device:TPU:0, one launch (start us, length us, event | category | flops | bytes accessed | tf_op | source)
XLA Modules:
  0.0 36.8 jit_solution(11014118144246001974)
XLA Ops:
  0.6 0.5 %collective-permute-start = (bf16[256,256]{1,0:T(8,128)(2,1)}, bf16[256,256]{1,0:T(8,128)(2,1)S(1)}, u32[]{:S(2)}, u32[]{:S(2)}) collective-permute-start(bf16[256,256]{1,0:T(8,128)(2,1)} %refs_0_.1), channel_id=1, source_target_pairs={{0,1},{1,0},{2,3},{3,2},{4,5},{5,4},{6,7},{7,6},{8,9},{9,8},{10,11... | collective-permute-start | bytes 393224 | tf_op jit(solution)/shard_map/ppermute | solution.py:194
  1.1 2.6 %collective-permute-start.1 = (bf16[256,256]{1,0:T(8,128)(2,1)}, bf16[256,256]{1,0:T(8,128)(2,1)S(1)}, u32[]{:S(2)}, u32[]{:S(2)}) collective-permute-start(bf16[256,256]{1,0:T(8,128)(2,1)} %refs_0_.1), channel_id=1, source_target_pairs={{0,2},{1,3},{2,0},{3,1},{4,6},{5,7},{6,4},{7,5},{8,10},{9,11},{10,... | collective-permute-start | bytes 393224 | tf_op jit(solution)/shard_map/ppermute | solution.py:194
  3.7 0.1 collective-permute-start.2
  4.5 0.0 copy-start
  4.5 1.2 %copy-done = bf16[2048,256]{1,0:T(8,128)(2,1)S(1)} copy-done((bf16[2048,256]{1,0:T(8,128)(2,1)S(1)}, bf16[2048,256]{1,0:T(8,128)(2,1)}, u32[]{:S(2)}) %copy-start) | copy-done | bytes 1048600
  5.7 0.0 copy-start.1
  5.7 0.0 copy-start.2
  5.7 0.0 copy-start.3
  5.7 1.4 %stage.1 = (bf16[2048,256]{1,0:T(8,128)(2,1)S(1)}, bf16[16,256,128]{2,1,0:T(8,128)(2,1)S(1)}, bf16[128,128,128]{2,1,0:T(8,128)(2,1)S(1)}, bf16[128,128,128]{2,1,0:T(8,128)(2,1)S(1)}) custom-call(s32[1]{0:T(128)S(6)} %copy.9.count_ref, bf16[2048,256]{1,0:T(8,128)(2,1)S(1)} %copy-done, bf16[1,128,128,128]{3,2,1,0:T(8,128)(2,1)} %rating_ref.1, ...), custom_call_target="tpu_custom_call" | custom-call | bytes 18000000 | tf_op jit(solution)/shard_map/stage/pallas_call | solution.py:206
  7.1 0.1 pad_add_fusion.place_ref
  7.2 0.0 collective-permute-done.refs_1_
  7.2 1.1 %collective-permute-done.1.refs_2_ = bf16[256,256]{1,0:T(8,128)(2,1)S(1)} collective-permute-done((bf16[256,256]{1,0:T(8,128)(2,1)}, bf16[256,256]{1,0:T(8,128)(2,1)S(1)}, u32[]{:S(2)}, u32[]{:S(2)}) %collective-permute-start.1) | collective-permute-done | bytes 131104 | tf_op jit(solution)/shard_map/ppermute | solution.py:194
  8.3 2.3 %collective-permute-done.2.refs_3_ = bf16[256,256]{1,0:T(8,128)(2,1)S(1)} collective-permute-done((bf16[256,256]{1,0:T(8,128)(2,1)}, bf16[256,256]{1,0:T(8,128)(2,1)S(1)}, u32[]{:S(2)}, u32[]{:S(2)}) %collective-permute-start.2) | collective-permute-done | bytes 131104 | tf_op jit(solution)/shard_map/ppermute | solution.py:194
  10.6 0.0 copy-done.1
  10.6 0.0 copy-done.2
  10.6 0.0 copy-done.3
  10.6 3.0 %item_sums.1 = (f32[512,256]{1,0:T(8,128)S(1)}, f32[512,256]{1,0:T(8,128)S(1)}, bf16[128,128,128]{2,1,0:T(8,128)(2,1)S(1)}, bf16[1024,256]{1,0:T(8,128)(2,1)S(1)}) custom-call(s32[1]{0:T(128)S(6)} %copy.9.count_ref, s32[2]{0:T(128)S(1)} %pad_add_fusion.place_ref, s32[1,128]{1,0:T(1,128)S(1)} %copy-done.2, s32[1,128]{1,0:T(1,128)S(1)} %copy-done.3, ...), custom_call_target="tpu_custom_call" | custom-call | bytes 24000000 | tf_op jit(solution)/shard_map/item_sums/pallas_call | solution.py:222
  13.6 2.8 %collective-permute-start.3 = (f32[512,256]{1,0:T(8,128)S(1)}, f32[512,256]{1,0:T(8,128)S(1)}, u32[]{:S(2)}, u32[]{:S(2)}) collective-permute-start(f32[512,256]{1,0:T(8,128)S(1)} %get-tuple-element.29), channel_id=1, source_target_pairs={{0,1},{1,0},{2,3},{3,2},{4,5},{5,4},{6,7},{7,6},{8,9},{9,8},{10,11... | collective-permute-start | bytes 1572872 | tf_op jit(solution)/shard_map/ppermute | solution.py:194
  16.4 1.5 %collective-permute-done.3.refs_1_ = f32[512,256]{1,0:T(8,128)S(1)} collective-permute-done((f32[512,256]{1,0:T(8,128)S(1)}, f32[512,256]{1,0:T(8,128)S(1)}, u32[]{:S(2)}, u32[]{:S(2)}) %collective-permute-start.3) | collective-permute-done | bytes 524320 | tf_op jit(solution)/shard_map/ppermute | solution.py:194
  17.9 0.1 sum_parts.2
  18.0 0.2 collective-permute-start.4
  18.2 4.3 %collective-permute-start.5 = (f32[128,256]{1,0:T(8,128)S(1)}, f32[128,256]{1,0:T(8,128)S(1)}, u32[]{:S(2)}, u32[]{:S(2)}) collective-permute-start(f32[128,256]{1,0:T(8,128)S(1)} %get-tuple-element.32), channel_id=1, source_target_pairs={{0,4},{1,5},{2,6},{3,7},{4,0},{5,1},{6,2},{7,3},{8,12},{9,13},{10,... | collective-permute-start | bytes 393224 | tf_op jit(solution)/shard_map/ppermute | solution.py:194
  22.5 0.0 collective-permute-start.6
  22.5 2.9 %user_sums.1 = (f32[2048,256]{1,0:T(8,128)}, f32[8,128]{1,0:T(8,128)S(1)}) custom-call(s32[1]{0:T(128)S(6)} %copy.9.count_ref, s32[2]{0:T(128)S(1)} %pad_add_fusion.place_ref, s32[1,128]{1,0:T(1,128)S(1)} %copy-done.2, s32[1,128]{1,0:T(1,128)S(1)} %copy-done.3, bf16[2048,256]{1,0:T(8,128)(2,1)S(1)} %get-tuple-element.20.user_ref, ...), custom_call_target="tpu_custom_call" | custom-call | bytes 15000000 | tf_op jit(solution)/shard_map/user_sums/pallas_call | solution.py:233
  25.4 0.0 collective-permute-done.4.refs_1_
  25.4 3.7 %collective-permute-done.5.refs_2_ = f32[128,256]{1,0:T(8,128)S(1)} collective-permute-done((f32[128,256]{1,0:T(8,128)S(1)}, f32[128,256]{1,0:T(8,128)S(1)}, u32[]{:S(2)}, u32[]{:S(2)}) %collective-permute-start.5) | collective-permute-done | bytes 131104 | tf_op jit(solution)/shard_map/ppermute | solution.py:194
  29.1 0.0 collective-permute-done.6.refs_3_
  29.1 2.1 %collective-permute-start.7 = (f32[32,256]{1,0:T(8,128)S(1)}, f32[32,256]{1,0:T(8,128)S(1)}, u32[]{:S(2)}, u32[]{:S(2)}) collective-permute-start(f32[32,256]{1,0:T(8,128)S(1)} %get-tuple-element.35), channel_id=1, source_target_pairs={{0,24},{1,25},{2,26},{3,27},{4,28},{5,29},{6,30},{7,31},{8,16},{9,... | collective-permute-start | bytes 98312 | tf_op jit(solution)/shard_map/ppermute | solution.py:194
  31.3 0.6 %collective-permute-start.8 = (f32[32,256]{1,0:T(8,128)S(1)}, f32[32,256]{1,0:T(8,128)S(1)}, u32[]{:S(2)}, u32[]{:S(2)}) collective-permute-start(f32[32,256]{1,0:T(8,128)S(1)} %get-tuple-element.36), channel_id=1, source_target_pairs={{0,16},{1,17},{2,18},{3,19},{4,20},{5,21},{6,22},{7,23},{8,24},{9,... | collective-permute-start | bytes 98312 | tf_op jit(solution)/shard_map/ppermute | solution.py:194
  31.9 1.7 %collective-permute-start.9 = (f32[32,256]{1,0:T(8,128)S(1)}, f32[32,256]{1,0:T(8,128)S(1)}, u32[]{:S(2)}, u32[]{:S(2)}) collective-permute-start(f32[32,256]{1,0:T(8,128)S(1)} %get-tuple-element.37), channel_id=1, source_target_pairs={{0,8},{1,9},{2,10},{3,11},{4,12},{5,13},{6,14},{7,15},{8,0},{9,1},... | collective-permute-start | bytes 98312 | tf_op jit(solution)/shard_map/ppermute | solution.py:194
  33.6 1.6 %collective-permute-done.7 = f32[32,256]{1,0:T(8,128)S(1)} collective-permute-done((f32[32,256]{1,0:T(8,128)S(1)}, f32[32,256]{1,0:T(8,128)S(1)}, u32[]{:S(2)}, u32[]{:S(2)}) %collective-permute-start.7) | collective-permute-done | bytes 32800 | tf_op jit(solution)/shard_map/ppermute | solution.py:194
  35.1 1.0 %collective-permute-done.8 = f32[32,256]{1,0:T(8,128)S(1)} collective-permute-done((f32[32,256]{1,0:T(8,128)S(1)}, f32[32,256]{1,0:T(8,128)S(1)}, u32[]{:S(2)}, u32[]{:S(2)}) %collective-permute-start.8) | collective-permute-done | bytes 32800 | tf_op jit(solution)/shard_map/ppermute | solution.py:194
  36.1 0.1 collective-permute-done.9
  36.2 0.6 %multiply_add_fusion = f32[32,256]{1,0:T(8,128)} fusion(f32[32,256]{1,0:T(8,128)S(1)} %collective-permute-done.9, f32[32,256]{1,0:T(8,128)S(1)} %collective-permute-done.8, f32[32,256]{1,0:T(8,128)S(1)} %get-tuple-element.34, f32[32,256]{1,0:T(8,128)S(1)} %collective-permute-done.7, bf16[256,256]{1,0:T(8,128)(2,1)S(1)} %copy-done.1, s32[]{:T(128)S(6)} %select_n.46, ...), kind=kLoop, calls=%fused_computation | loop fusion | flops 81920 | bytes 229383 | tf_op jit(solution)/shard_map/add | solution.py:259
  (2 shorter events, 0.0 us)
Async XLA Ops:
  0.6 6.6 %collective-permute-start = (bf16[256,256]{1,0:T(8,128)(2,1)}, bf16[256,256]{1,0:T(8,128)(2,1)S(1)}, u32[]{:S(2)}, u32[]{:S(2)}) collective-permute-start(bf16[256,256]{1,0:T(8,128)(2,1)} %refs_0_.1), channel_id=1, source_target_pairs={{0,1},{1,0},{2,3},{3,2},{4,5},{5,4},{6,7},{7,6},{8,9},{9,8},{10,11... | collective-permute-start | bytes 393224 | tf_op jit(solution)/shard_map/ppermute | solution.py:194
  1.1 7.2 %collective-permute-start.1 = (bf16[256,256]{1,0:T(8,128)(2,1)}, bf16[256,256]{1,0:T(8,128)(2,1)S(1)}, u32[]{:S(2)}, u32[]{:S(2)}) collective-permute-start(bf16[256,256]{1,0:T(8,128)(2,1)} %refs_0_.1), channel_id=1, source_target_pairs={{0,2},{1,3},{2,0},{3,1},{4,6},{5,7},{6,4},{7,5},{8,10},{9,11},{10,... | collective-permute-start | bytes 393224 | tf_op jit(solution)/shard_map/ppermute | solution.py:194
  3.7 6.8 %collective-permute-start.2 = (bf16[256,256]{1,0:T(8,128)(2,1)}, bf16[256,256]{1,0:T(8,128)(2,1)S(1)}, u32[]{:S(2)}, u32[]{:S(2)}) collective-permute-start(bf16[256,256]{1,0:T(8,128)(2,1)} %refs_0_.1), channel_id=1, source_target_pairs={{0,3},{1,2},{2,1},{3,0},{4,7},{5,6},{6,5},{7,4},{8,11},{9,10},{10,... | collective-permute-start | bytes 393224 | tf_op jit(solution)/shard_map/ppermute | solution.py:194
  4.5 1.2 %copy-start = (bf16[2048,256]{1,0:T(8,128)(2,1)S(1)}, bf16[2048,256]{1,0:T(8,128)(2,1)}, u32[]{:S(2)}) copy-start(bf16[2048,256]{1,0:T(8,128)(2,1)} %user_ref.1) | copy-start | bytes 3145732
  5.7 4.9 %copy-start.1 = (bf16[256,256]{1,0:T(8,128)(2,1)S(1)}, bf16[256,256]{1,0:T(8,128)(2,1)}, u32[]{:S(2)}) copy-start(bf16[256,256]{1,0:T(8,128)(2,1)} %refs_0_.1) | copy-start | bytes 393220
  5.7 4.9 %copy-start.2 = (s32[1,128]{1,0:T(1,128)S(1)}, s32[1,128]{1,0:T(1,128)}, u32[]{:S(2)}) copy-start(s32[1,128]{1,0:T(1,128)} %user_id_ref.3) | copy-start | bytes 1540
  5.7 4.9 %copy-start.3 = (s32[1,128]{1,0:T(1,128)S(1)}, s32[1,128]{1,0:T(1,128)}, u32[]{:S(2)}) copy-start(s32[1,128]{1,0:T(1,128)} %item_id_ref.3) | copy-start | bytes 1540
  13.6 4.3 %collective-permute-start.3 = (f32[512,256]{1,0:T(8,128)S(1)}, f32[512,256]{1,0:T(8,128)S(1)}, u32[]{:S(2)}, u32[]{:S(2)}) collective-permute-start(f32[512,256]{1,0:T(8,128)S(1)} %get-tuple-element.29), channel_id=1, source_target_pairs={{0,1},{1,0},{2,3},{3,2},{4,5},{5,4},{6,7},{7,6},{8,9},{9,8},{10,11... | collective-permute-start | bytes 1572872 | tf_op jit(solution)/shard_map/ppermute | solution.py:194
  18.0 7.4 %collective-permute-start.4 = (f32[128,256]{1,0:T(8,128)S(1)}, f32[128,256]{1,0:T(8,128)S(1)}, u32[]{:S(2)}, u32[]{:S(2)}) collective-permute-start(f32[128,256]{1,0:T(8,128)S(1)} %get-tuple-element.31), channel_id=1, source_target_pairs={{0,6},{1,7},{2,4},{3,5},{4,2},{5,3},{6,0},{7,1},{8,14},{9,15},{10,... | collective-permute-start | bytes 393224 | tf_op jit(solution)/shard_map/ppermute | solution.py:194
  18.2 10.9 %collective-permute-start.5 = (f32[128,256]{1,0:T(8,128)S(1)}, f32[128,256]{1,0:T(8,128)S(1)}, u32[]{:S(2)}, u32[]{:S(2)}) collective-permute-start(f32[128,256]{1,0:T(8,128)S(1)} %get-tuple-element.32), channel_id=1, source_target_pairs={{0,4},{1,5},{2,6},{3,7},{4,0},{5,1},{6,2},{7,3},{8,12},{9,13},{10,... | collective-permute-start | bytes 393224 | tf_op jit(solution)/shard_map/ppermute | solution.py:194
  22.5 6.6 %collective-permute-start.6 = (f32[128,256]{1,0:T(8,128)S(1)}, f32[128,256]{1,0:T(8,128)S(1)}, u32[]{:S(2)}, u32[]{:S(2)}) collective-permute-start(f32[128,256]{1,0:T(8,128)S(1)} %get-tuple-element.33), channel_id=1, source_target_pairs={{0,2},{1,3},{2,0},{3,1},{4,6},{5,7},{6,4},{7,5},{8,10},{9,11},{10,... | collective-permute-start | bytes 393224 | tf_op jit(solution)/shard_map/ppermute | solution.py:194
  29.1 6.0 %collective-permute-start.7 = (f32[32,256]{1,0:T(8,128)S(1)}, f32[32,256]{1,0:T(8,128)S(1)}, u32[]{:S(2)}, u32[]{:S(2)}) collective-permute-start(f32[32,256]{1,0:T(8,128)S(1)} %get-tuple-element.35), channel_id=1, source_target_pairs={{0,24},{1,25},{2,26},{3,27},{4,28},{5,29},{6,30},{7,31},{8,16},{9,... | collective-permute-start | bytes 98312 | tf_op jit(solution)/shard_map/ppermute | solution.py:194
  31.3 4.9 %collective-permute-start.8 = (f32[32,256]{1,0:T(8,128)S(1)}, f32[32,256]{1,0:T(8,128)S(1)}, u32[]{:S(2)}, u32[]{:S(2)}) collective-permute-start(f32[32,256]{1,0:T(8,128)S(1)} %get-tuple-element.36), channel_id=1, source_target_pairs={{0,16},{1,17},{2,18},{3,19},{4,20},{5,21},{6,22},{7,23},{8,24},{9,... | collective-permute-start | bytes 98312 | tf_op jit(solution)/shard_map/ppermute | solution.py:194
  31.9 4.3 %collective-permute-start.9 = (f32[32,256]{1,0:T(8,128)S(1)}, f32[32,256]{1,0:T(8,128)S(1)}, u32[]{:S(2)}, u32[]{:S(2)}) collective-permute-start(f32[32,256]{1,0:T(8,128)S(1)} %get-tuple-element.37), channel_id=1, source_target_pairs={{0,8},{1,9},{2,10},{3,11},{4,12},{5,13},{6,14},{7,15},{8,0},{9,1},... | collective-permute-start | bytes 98312 | tf_op jit(solution)/shard_map/ppermute | solution.py:194
